TPU v7x, 32 devices: a whole 2x2x4 slice. The times are simulated.
32 devices in a mesh: groups: 2 (over x), planes: 4 (over y, core), chan: 4 (over z).
Axes of the slice: x: 2, y: 2, z: 4, core: 2. Of those that a mesh axis runs over, the one named last changes fastest.
Arguments:
- field: float32 [2, 16, 128, 128, 128], P('groups', None, ('planes', 'chan')), parts along dimension 0, may hold values from -6 to 6
- cotangent: float32 [2, 16, 128, 128, 128], P('groups', None, ('planes', 'chan')), parts along dimension 0, may hold values from -6 to 6
- spec_weight: float32 [2, 16, 16, 64, 2048], P(None, None, None, 'planes', 'chan'), may hold values from -1.5 to 1.5
- point_weight: float32 [16, 16], replicated, may hold values from -1.5 to 1.5
- bias: float32 [16], replicated, may hold values from -3 to 3
Outputs:
- output: float32 [2, 16, 128, 128, 128], P('groups', None, ('planes', 'chan')), parts along dimension 0
- field_grad: float32 [2, 16, 128, 128, 128], P('groups', None, ('planes', 'chan')), parts along dimension 0
- weight_grad: float32 [4, 16, 16, 64, 2048], P('groups', None, None, 'planes', 'chan'), parts along dimension 0
There are 2 independent parts, one for each index of `groups`. A program takes and returns all parts, laid end to end along the dimension named above; an argument that names none is the same for every part. Nothing has to cross between parts.
All inputs are finite; a program needn't handle non-finite values.
Results may differ from a plain program's by a relative error of at most 0.0001.
Values sent between devices are 32-bit elements; how exact they have to be, the bound alone decides.
A program may use at most 192 MiB of HBM per device.

v0:
```python
import math

import jax
import jax.numpy as jnp
from jax import lax
from jax.sharding import PartitionSpec as P

GX = 128
GY = 128
GZ = 128
MODES = 32


exact_mode = lax.Precision.HIGHEST


def retained(length):
    indices = jnp.arange(2 * MODES)
    return jnp.where(indices < MODES, indices, length - 2 * MODES + indices)


def phase_table(positions, freqs, length):
    turn_count = positions[:, None] * freqs[None, :] % length
    angles = turn_count.astype(jnp.float32) * (2.0 * math.pi / length)
    return (jnp.cos(angles), jnp.sin(angles))


def analysis(field):
    batch_size, channels, local_planes, second_length, third_length = field.shape
    plane_count = lax.axis_size("planes")
    channel_groups = lax.axis_size("chan")
    group_width = channels // channel_groups
    local_modes = 2 * MODES // plane_count
    first_length = local_planes * plane_count * channel_groups
    cosine, sine_part = phase_table(
        jnp.arange(second_length), retained(second_length), second_length
    )
    second_table = jnp.stack([cosine, -sine_part], 1).reshape(
        second_length, 2, plane_count, local_modes
    )
    cosine, sine_part = phase_table(jnp.arange(third_length), jnp.arange(MODES), third_length)
    third_table = jnp.stack(
        [jnp.stack([cosine, -sine_part], 1), jnp.stack([sine_part, cosine], 1)], 0
    )
    grouped = field.reshape(
        batch_size, channel_groups, group_width, local_planes, second_length, third_length
    )
    second_pass = jnp.einsum("bcdxyz,yspk->bcdxspkz", grouped, second_table, precision=exact_mode)
    spectra = jnp.einsum("bcdxspkz,sztm->bpckxdtm", second_pass, third_table, precision=exact_mode)
    spectra = spectra.reshape(
        batch_size, plane_count * channel_groups, local_modes, local_planes, group_width * 2 * MODES
    )
    arrived = lax.all_to_all(spectra, ("planes", "chan"), split_axis=1, concat_axis=3, tiled=True)
    positions = jnp.arange(first_length)
    arrived = arrived.reshape(batch_size, local_modes, first_length, group_width, 2, MODES)
    cosine, sine_part = phase_table(positions, retained(first_length), first_length)
    first_table = jnp.stack(
        [jnp.stack([cosine, -sine_part], 1), jnp.stack([sine_part, cosine], 1)], 1
    )
    first_pass = jnp.einsum("bkxdsm,xstf->bkdtfm", arrived, first_table, precision=exact_mode)
    first_pass = first_pass.reshape(batch_size, local_modes, group_width, 2, 2 * MODES * MODES)
    return lax.all_to_all(first_pass, "chan", split_axis=4, concat_axis=2, tiled=True)


def synthesis(spectrum):
    batch_size, local_modes, channels = (spectrum.shape[0], spectrum.shape[1], spectrum.shape[2])
    plane_count = lax.axis_size("planes")
    channel_groups = lax.axis_size("chan")
    group_width = channels // channel_groups
    local_planes = GX // (plane_count * channel_groups)
    gathered = lax.all_to_all(spectrum, "chan", split_axis=2, concat_axis=4, tiled=True)
    gathered = gathered.reshape(batch_size, local_modes, group_width, 2, 2 * MODES, MODES)
    cosine, sine_part = phase_table(jnp.arange(GX), retained(GX), GX)
    cosine_t = cosine.T
    sine_t = sine_part.T
    first_inverse = jnp.stack(
        [jnp.stack([cosine_t, sine_t], -1), jnp.stack([-sine_t, cosine_t], -1)], 0
    )
    first_pass = jnp.einsum("bkdsfm,sfxt->bkxdtm", gathered, first_inverse, precision=exact_mode)
    first_pass = first_pass.reshape(batch_size, local_modes, GX, group_width * 2 * MODES)
    returned = lax.all_to_all(
        first_pass[:, None], ("planes", "chan"), split_axis=3, concat_axis=1, tiled=True
    )
    returned = returned.reshape(
        batch_size, plane_count, channel_groups, local_modes, local_planes, group_width, 2, MODES
    )
    source_form = "bpckxdtm"
    cosine, sine_part = phase_table(jnp.arange(GZ), jnp.arange(MODES), GZ)
    cosine_t = cosine.T
    sine_t = sine_part.T
    third_inverse = jnp.stack(
        [jnp.stack([cosine_t, sine_t], 1), jnp.stack([-sine_t, cosine_t], 1)], 0
    )
    depth_pass = jnp.einsum(
        source_form + ",tmuz->bcdxpkuz", returned, third_inverse, precision=exact_mode
    )
    cosine, sine_part = phase_table(jnp.arange(GY), retained(GY), GY)
    second_inverse = jnp.stack([cosine.T, -sine_part.T], 0).reshape(2, plane_count, local_modes, GY)
    physical = jnp.einsum("bcdxpkuz,upky->bcdxyz", depth_pass, second_inverse, precision=exact_mode)
    return physical.reshape(batch_size, channels, local_planes, GY, GZ)


def by_sample(function, values):
    result = function(values)
    return result


def mode_weighting(mode_count):
    depth_mode = jnp.arange(mode_count) % MODES
    return jnp.where(depth_mode == 0, 1.0, 2.0).astype(jnp.float32) / float(GX * GY * GZ)


def contract(operand, weights):
    return jnp.einsum("bkin,iokn->bkon", operand, weights, precision=exact_mode)


def adjoint(operand, weights):
    return jnp.einsum("bkon,iokn->bkin", operand, weights, precision=exact_mode)


def outer_sum(first_operand, second_operand):
    return jnp.einsum("bkin,bkon->iokn", first_operand, second_operand, precision=exact_mode)


def local(field, cotangent, spec_weight, point_weight, bias):
    spectrum = by_sample(analysis, field)
    weight_re = spec_weight[0]
    weight_im = spec_weight[1]
    spec_re = spectrum[:, :, :, 0]
    spec_im = spectrum[:, :, :, 1]
    weighting = mode_weighting(spectrum.shape[-1])
    mixed_re = (contract(spec_re, weight_re) - contract(spec_im, weight_im)) * weighting
    mixed_im = (contract(spec_re, weight_im) + contract(spec_im, weight_re)) * weighting
    mixed_modes = jnp.stack([mixed_re, mixed_im], 3)
    spectral = by_sample(synthesis, mixed_modes)
    pointwise = jnp.einsum("bixyz,io->boxyz", field, point_weight, precision=exact_mode)
    preactivation = spectral + pointwise + bias[None, :, None, None, None]
    normal_cdf = 0.5 * (1.0 + lax.erf(preactivation * (1.0 / math.sqrt(2.0))))
    output = preactivation * normal_cdf
    derivative = normal_cdf + preactivation * jnp.exp(-0.5 * preactivation * preactivation) * (
        1.0 / math.sqrt(2.0 * math.pi)
    )
    pre_grad = cotangent * derivative
    raw_grad = by_sample(analysis, pre_grad)
    grad_re = raw_grad[:, :, :, 0] * weighting
    grad_im = raw_grad[:, :, :, 1] * weighting
    spectrum_grad = jnp.stack(
        [
            adjoint(grad_re, weight_re) + adjoint(grad_im, weight_im),
            adjoint(grad_im, weight_re) - adjoint(grad_re, weight_im),
        ],
        3,
    )
    weight_grad = jnp.stack(
        [
            outer_sum(spec_re, grad_re) + outer_sum(spec_im, grad_im),
            outer_sum(spec_re, grad_im) - outer_sum(spec_im, grad_re),
        ],
        0,
    )
    local_grad = jnp.einsum("boxyz,io->bixyz", pre_grad, point_weight, precision=exact_mode)
    field_grad = local_grad + by_sample(synthesis, spectrum_grad)
    return (output, field_grad, weight_grad)


def solution(mesh):
    in_specs = (
        P("groups", None, ("planes", "chan"), None, None),
        P("groups", None, ("planes", "chan"), None, None),
        P(None, None, None, "planes", "chan"),
        P(),
        P(),
    )
    out_specs = (
        P("groups", None, ("planes", "chan"), None, None),
        P("groups", None, ("planes", "chan"), None, None),
        P("groups", None, None, "planes", "chan"),
    )
    return jax.shard_map(local, mesh=mesh, in_specs=in_specs, out_specs=out_specs, check_vma=False)
```

profile of v0, /device:TPU:0, one launch (start us, length us, event | category | flops | bytes accessed | tf_op | source)
XLA Modules:
  0.0 735.8 jit_solution(8426604456952516511)
XLA Ops:
  1.1 10.2 %convolution_bitcast_fusion = f32[4,4,8,2,4,16,128]{6,5,2,1,0,4,3:T(8,128)S(1)} fusion(f32[4,4,8,128,128,1,1]{4,3,2,1,0,6,5:T(8,128)} %bitcast.393, f32[128,1,4,16]{0,3,2,1:T(8,128)S(1)} %get-tuple-element.50, f32[128,1,4,16]{0,3,2,1:T(8,128)S(1)} %get-tuple-element.49), kind=kOutput, calls=%fused_computation.63 | convolution fusion | flops 3221241856 | bytes 16842752 | tf_op jit(solution)/shard_map/bcdxyz,yspk->bcdxspkz/dot_general | solution.py:48
  11.3 7.1 fusion.49
  18.5 8.0 %copy.104 = f32[1,4,4,16,8,4,2,32]{7,6,5,4,3,2,1,0:T(2,128)} copy(f32[1,4,4,16,8,4,2,32]{7,3,1,4,5,2,6,0:T(8,128)S(1)} %fusion.49) | data formatting | bytes 4194304 | tf_op jit(solution)/shard_map/bcdxspkz,sztm->bpckxdtm/transpose | solution.py:49
  26.4 12.4 %reshape.755 = f32[1,16,16,8,256]{4,3,2,1,0:T(8,128)} reshape(f32[1,4,4,16,8,4,2,32]{7,6,5,4,3,2,1,0:T(2,128)} %copy.104) | data formatting | bytes 4194304 | tf_op jit(solution)/shard_map/reshape | solution.py:50
  38.8 7.4 %all-to-all-start = ((f32[1,16,16,8,256]{4,3,2,0,1:T(8,128)}), f32[1,16,16,8,256]{4,3,2,0,1:T(8,128)S(1)}, u32[]{:S(2)}, u32[]{:S(2)}) async-start(f32[1,16,16,8,256]{4,3,2,0,1:T(8,128)} %bitcast.51), calls=%async_computation | async-start | bytes 4194304 | tf_op jit(solution)/shard_map/all_to_all | solution.py:53
  46.5 49.2 %all-to-all-done = f32[1,16,16,8,256]{4,3,2,0,1:T(8,128)S(1)} async-done(((f32[1,16,16,8,256]{4,3,2,0,1:T(8,128)}), f32[1,16,16,8,256]{4,3,2,0,1:T(8,128)S(1)}, u32[]{:S(2)}, u32[]{:S(2)}) %all-to-all-start) | async-done | bytes 2097184 | tf_op jit(solution)/shard_map/all_to_all | solution.py:53
  95.7 1.3 copy-done.2
  97.0 1.8 copy.106
  98.8 8.3 %reshape.756 = f32[16,128,4,2,32]{4,3,2,1,0:T(2,128)} reshape(f32[1,1,16,16,8,256]{5,4,3,2,1,0:T(8,128)S(1)} %copy.106) | data formatting | bytes 4194304 | tf_op jit(solution)/shard_map/reshape.5
  107.1 10.2 %copy.107 = f32[16,128,4,2,32]{1,4,3,2,0:T(8,128)S(1)} copy(f32[16,128,4,2,32]{4,3,2,1,0:T(2,128)} %reshape.756) | data formatting | bytes 4194304 | tf_op jit(solution)/shard_map/reshape.5
  117.3 3.2 fusion.68
  120.4 12.0 %copy.225 = f32[1,16,4,2,64,32]{1,3,2,5,4,0:T(2,128)} copy(f32[1,16,4,2,64,32]{4,5,2,1,3,0:T(8,128)} %fusion.68) | data formatting | bytes 2097152 | tf_op jit(solution)/shard_map/reshape | solution.py:61
  132.4 13.5 %reshape.821 = f32[4,1,65536]{2,1,0:T(1,128)} reshape(f32[2048,1,4,2,16]{4,3,2,1,0:T(2,128)} %bitcast.388) | data formatting | bytes 2097152
  145.9 3.7 all-to-all-start.1
  149.6 25.8 %all-to-all-done.1 = f32[4,1,65536]{2,1,0:T(1,128)S(1)} async-done(((f32[4,1,65536]{2,1,0:T(1,128)}), f32[4,1,65536]{2,1,0:T(1,128)S(1)}, u32[]{:S(2)}, u32[]{:S(2)}) %all-to-all-start.1) | async-done | bytes 1048608 | tf_op jit(solution)/shard_map/all_to_all | solution.py:62
  176.0 3.7 reduce.16
  179.8 14.3 %reshape.822 = f32[2048,1,4,2,16]{4,3,2,1,0:T(2,128)} reshape(f32[4,65536]{1,0:T(4,128)S(1)} %reduce.16) | data formatting | bytes 2097152
  194.1 10.2 %copy.226 = f32[1,16,4,2,4,512]{5,4,1,3,2,0:T(4,128)S(1)} copy(f32[1,16,4,2,4,512]{1,3,2,5,4,0:T(2,128)} %bitcast.390) | data formatting | bytes 2097152 | tf_op jit(solution)/shard_map/all_to_all | solution.py:62
  204.8 7.4 %fusion.23 = (f32[16,512,16]{1,0,2:T(8,128)S(1)}, f32[16,512,16]{1,0,2:T(8,128)S(1)}, f32[16,512,16]{1,0,2:T(8,128)S(1)}, f32[16,512,16]{1,0,2:T(8,128)S(1)}) fusion(f32[2,16,16,16,512]{4,3,2,1,0:T(8,128)} %param.7, f32[16,512,16]{1,0,2:T(8,128)S(1)} %get-tuple-element.36, f32[16,512,16]{1,0,2:T(8,128)S(1)} %get-tuple-element.35), kind=kLoop, calls=%fused_computation.32 | loop fusion | flops 16252928 | bytes 19922944 | tf_op jit(solution)/shard_map/bkin,iokn->bkon/dot_general | solution.py:114
  212.5 1.0 pad_maximum_fusion.1
  213.6 3.5 all-to-all-start.2
  217.3 25.0 %all-to-all-done.2 = f32[1,16,16,2,512]{4,1,3,0,2:T(8,128)S(1)} async-done(((f32[1,16,16,2,512]{4,1,3,0,2:T(8,128)}), f32[1,16,16,2,512]{4,1,3,0,2:T(8,128)S(1)}, u32[]{:S(2)}, u32[]{:S(2)}) %all-to-all-start.2) | async-done | bytes 1048608 | tf_op jit(solution)/shard_map/all_to_all | solution.py:71
  243.0 2.7 reshape.760
  245.6 9.1 %fusion.74 = f32[1,16,128,4,2,32]{2,5,3,1,4,0:T(8,128)S(1)} fusion(f32[16,4,2,64,32]{4,3,2,1,0:T(8,128)} %reshape.760, f32[1,64,128,2]{2,1,0,3:T(8,128)S(1)} %get-tuple-element.38, f32[1,64,128,2]{2,1,0,3:T(8,128)S(1)} %get-tuple-element.37), kind=kOutput, calls=%fused_computation.73 | convolution fusion | flops 805339136 | bytes 3276800 | tf_op jit(solution)/shard_map/bkdsfm,sfxt->bkxdtm/dot_general | solution.py:79
  254.9 2.0 copy.116
  256.9 4.8 all-to-all-start.3
  262.0 0.8 fusion.125
  262.8 48.4 %all-to-all-done.3 = f32[1,1,16,128,256]{4,2,1,0,3:T(8,128)} async-done(((f32[1,1,16,128,256]{4,2,1,0,3:T(8,128)}), f32[1,1,16,128,256]{4,2,1,0,3:T(8,128)}, u32[]{:S(2)}, u32[]{:S(2)}) %all-to-all-start.3) | async-done | bytes 2097184 | tf_op jit(solution)/shard_map/all_to_all | solution.py:81
  311.2 2.8 copy.292
  314.0 8.3 %reshape.819 = f32[4,4,16,8,4,2,32]{6,5,4,3,1,0,2:T(2,128)} reshape(f32[1,16,1,16,8,256]{5,4,1,3,2,0:T(8,128)S(1)} %bitcast.400) | data formatting | bytes 4194304 | tf_op jit(solution)/shard_map/reshape.42
  322.3 14.1 %fusion.52 = f32[4,4,8,4,16,2,128]{6,4,1,2,0,3,5:T(8,128)S(1)} fusion(f32[4,4,16,8,4,2,32]{6,5,4,3,1,0,2:T(2,128)} %reshape.819, f32[1,32,2,128]{3,1,0,2:T(8,128)S(1)} %get-tuple-element.42, f32[1,32,2,128]{3,1,0,2:T(8,128)S(1)} %get-tuple-element.41), kind=kOutput, calls=%fused_computation.60 | convolution fusion | flops 1610629120 | bytes 10551296 | tf_op jit(solution)/shard_map/bpckxdtm,tmuz->bcdxpkuz/dot_general | solution.py:94
  336.5 7.7 %fusion.35 = f32[128,4,4,8,128,1,1]{4,0,6,5,3,2,1:T(8,128)S(1)} fusion(f32[4,4,8,4,16,2,128]{6,4,1,2,0,3,5:T(8,128)S(1)} %fusion.52, f32[1,4,16,128]{3,2,0,1:T(8,128)S(1)} %copy-done.23, f32[1,4,16,128]{3,2,0,1:T(8,128)S(1)} %copy-done.21), kind=kOutput, calls=%fused_computation.47 | convolution fusion | flops 3221241856 | bytes 16842752 | tf_op jit(solution)/shard_map/bcdxpkuz,upky->bcdxyz/dot_general | solution.py:99
  344.3 22.0 %fusion.5 = (f32[1,16,8,128,128]{4,1,3,2,0:T(8,128)S(1)}, f32[16,8,128,128]{3,0,2,1:T(8,128)}) fusion(f32[1,16,8,128,128]{4,3,2,1,0:T(8,128)S(1)} %bitcast.408, f32[16]{0:T(128)S(1)} %copy-done.25, f32[16,8,128,128]{3,2,1,0:T(8,128)S(1)} %bitcast.396, f32[16,16]{1,0:T(8,128)S(1)} %copy-done, f32[16,8,128,128]{3,2,1,0:T(8,128)S(1)} %bitcast.397), kind=kOutput, calls=%fused_computation.7 | convolution fusion | flops 425721856 | bytes 41944128 | tf_op jit(solution)/shard_map/bixyz,io->boxyz/dot_general | solution.py:136
  366.3 11.7 %fusion.61 = f32[4,4,8,2,4,16,128]{6,5,2,1,0,4,3:T(8,128)S(1)} fusion(f32[4,4,8,128,128,1,1]{4,1,0,3,2,6,5:T(4,128)S(1)} %bitcast.387, f32[128,1,4,16]{0,3,2,1:T(8,128)} %copy-done.20, f32[128,1,4,16]{0,3,2,1:T(8,128)} %copy-done.19), kind=kOutput, calls=%fused_computation.64 | convolution fusion | flops 3221241856 | bytes 16842752 | tf_op jit(solution)/shard_map/bcdxyz,yspk->bcdxspkz/dot_general | solution.py:48
  378.0 7.3 fusion.55
  385.3 8.0 %copy.127 = f32[1,4,4,16,8,4,2,32]{7,6,5,4,3,2,1,0:T(2,128)} copy(f32[1,4,4,16,8,4,2,32]{7,3,1,4,5,2,6,0:T(8,128)S(1)} %fusion.55) | data formatting | bytes 4194304 | tf_op jit(solution)/shard_map/bcdxspkz,sztm->bpckxdtm/transpose | solution.py:49
  393.3 11.2 %reshape.768 = f32[1,16,16,8,256]{4,3,2,1,0:T(8,128)S(1)} reshape(f32[1,4,4,16,8,4,2,32]{7,6,5,4,3,2,1,0:T(2,128)} %copy.127) | data formatting | bytes 4194304 | tf_op jit(solution)/shard_map/reshape | solution.py:50
  404.5 52.5 %all_to_all.126 = f32[1,16,16,8,256]{4,3,2,0,1:T(8,128)S(1)} all-to-all(f32[1,16,16,8,256]{4,3,2,0,1:T(8,128)S(1)} %bitcast.401), channel_id=1, replica_groups=mesh['groups'=2,'planes'=4,'chan'=4] {'planes','chan'}, dimensions={1} | all-to-all | bytes 4194304 | tf_op jit(solution)/shard_map/all_to_all | solution.py:53
  457.2 8.3 %reshape.769 = f32[16,128,4,2,32]{4,3,2,1,0:T(2,128)} reshape(f32[1,1,16,16,8,256]{5,4,3,2,1,0:T(8,128)S(1)} %copy.129) | data formatting | bytes 4194304 | tf_op jit(solution)/shard_map/reshape.58
  465.5 10.2 %copy.130 = f32[16,128,4,2,32]{1,4,3,2,0:T(8,128)S(1)} copy(f32[16,128,4,2,32]{4,3,2,1,0:T(2,128)} %reshape.769) | data formatting | bytes 4194304 | tf_op jit(solution)/shard_map/reshape.58
  475.7 3.2 fusion.71
  478.9 12.0 %copy.233 = f32[1,16,4,2,64,32]{1,3,2,5,4,0:T(2,128)} copy(f32[1,16,4,2,64,32]{4,5,2,1,3,0:T(8,128)} %fusion.71) | data formatting | bytes 2097152 | tf_op jit(solution)/shard_map/reshape | solution.py:61
  490.8 12.8 %reshape.823 = f32[4,1,65536]{2,1,0:T(1,128)S(1)} reshape(f32[2048,1,4,2,16]{4,3,2,1,0:T(2,128)} %bitcast.389) | data formatting | bytes 2097152
  503.7 28.7 %all_to_all.127 = f32[4,1,65536]{2,1,0:T(1,128)S(1)} all-to-all(f32[4,1,65536]{2,1,0:T(1,128)S(1)} %reshape.823), channel_id=1, replica_groups=mesh['groups'=2,'planes'=4,'chan'=4] {'chan'}, dimensions={0} | all-to-all | bytes 2097152 | tf_op jit(solution)/shard_map/all_to_all | solution.py:62
  532.4 3.7 reduce.17
  536.1 14.3 %reshape.824 = f32[2048,1,4,2,16]{4,3,2,1,0:T(2,128)} reshape(f32[4,65536]{1,0:T(4,128)S(1)} %reduce.17) | data formatting | bytes 2097152
  550.4 10.3 %copy.234 = f32[1,16,4,2,4,512]{5,4,1,3,2,0:T(4,128)S(1)} copy(f32[1,16,4,2,4,512]{1,3,2,5,4,0:T(2,128)} %bitcast.391) | data formatting | bytes 2097152 | tf_op jit(solution)/shard_map/all_to_all | solution.py:62
  561.3 12.7 %add_bitcast_fusion = (f32[1,16,16,16,512]{4,3,2,1,0:T(8,128)}, f32[1,16,16,16,512]{4,3,2,1,0:T(8,128)}, f32[16,512,16]{1,0,2:T(8,128)S(1)}, f32[16,512,16]{1,0,...) fusion(f32[16,512,16]{1,0,2:T(8,128)S(1)} %get-tuple-element.30, ...), kind=kLoop, calls=%fused_computation.51 | loop fusion | flops 28835840 | bytes 37748736 | tf_op jit(solution)/shard_map/stack | solution.py:154
  574.2 27.7 %all_to_all.128 = f32[1,16,16,2,512]{4,1,3,0,2:T(8,128)S(1)} all-to-all(f32[1,16,16,2,512]{4,1,3,0,2:T(8,128)S(1)} %pad_maximum_fusion.2), channel_id=1, replica_groups=mesh['groups'=2,'planes'=4,'chan'=4] {'chan'}, dimensions={2} | all-to-all | bytes 2097152 | tf_op jit(solution)/shard_map/all_to_all | solution.py:71
  602.6 2.7 reshape.771
  605.3 9.1 %fusion.77 = f32[1,16,128,4,2,32]{2,5,3,1,4,0:T(8,128)S(1)} fusion(f32[16,4,2,64,32]{4,3,2,1,0:T(8,128)} %reshape.771, f32[1,64,128,2]{2,1,0,3:T(8,128)S(1)} %copy-done.10, f32[1,64,128,2]{2,1,0,3:T(8,128)S(1)} %copy-done.8), kind=kOutput, calls=%fused_computation.74 | convolution fusion | flops 805339136 | bytes 3276800 | tf_op jit(solution)/shard_map/bkdsfm,sfxt->bkxdtm/dot_general | solution.py:79
  614.6 2.0 copy.139
  616.6 4.6 all-to-all-start.7
  621.2 5.0 multiply_bitcast_fusion
  626.2 6.0 copy.145
  632.2 10.6 %pad_maximum_fusion = f32[2,16,16,16,512]{4,3,2,1,0:T(8,128)} fusion(f32[1,16,16,16,512]{4,3,2,1,0:T(8,128)} %get-tuple-element.28, f32[1,16,16,16,512]{4,3,2,1,0:T(8,128)S(1)} %bitcast.399), kind=kLoop, calls=%fused_computation | loop fusion | flops 4194304 | bytes 33554432 | tf_op jit(solution)/shard_map/stack | solution.py:154
  642.8 27.9 %all-to-all-done.7 = f32[1,1,16,128,256]{4,2,1,0,3:T(8,128)} async-done(((f32[1,1,16,128,256]{4,2,1,0,3:T(8,128)}), f32[1,1,16,128,256]{4,2,1,0,3:T(8,128)}, u32[]{:S(2)}, u32[]{:S(2)}) %all-to-all-start.7) | async-done | bytes 2097184 | tf_op jit(solution)/shard_map/all_to_all | solution.py:81
  670.6 2.8 copy.291
  673.5 8.3 %reshape.820 = f32[4,4,16,8,4,2,32]{6,5,4,3,1,0,2:T(2,128)} reshape(f32[1,16,1,16,8,256]{5,4,1,3,2,0:T(8,128)S(1)} %bitcast.402) | data formatting | bytes 4194304 | tf_op jit(solution)/shard_map/reshape.72
  681.7 13.8 %fusion.58 = f32[4,4,8,4,16,2,128]{6,4,1,2,0,3,5:T(8,128)S(1)} fusion(f32[4,4,16,8,4,2,32]{6,5,4,3,1,0,2:T(2,128)} %reshape.820, f32[1,32,2,128]{3,1,0,2:T(8,128)S(1)} %copy-done.18, f32[1,32,2,128]{3,1,0,2:T(8,128)S(1)} %copy-done.16), kind=kOutput, calls=%fused_computation.62 | convolution fusion | flops 1610629120 | bytes 10551296 | tf_op jit(solution)/shard_map/bpckxdtm,tmuz->bcdxpkuz/dot_general | solution.py:94
  695.5 10.0 %fusion.46 = f32[1,4,4,8,128,128]{5,4,3,2,1,0:T(8,128)} fusion(f32[4,4,8,4,16,2,128]{6,4,1,2,0,3,5:T(8,128)S(1)} %fusion.58, f32[1,4,16,128]{3,2,0,1:T(8,128)S(1)} %copy-done.24, f32[1,4,16,128]{3,2,0,1:T(8,128)S(1)} %copy-done.22), kind=kOutput, calls=%fused_computation.58 | convolution fusion | flops 3221241856 | bytes 16842752 | tf_op jit(solution)/shard_map/bcdxpkuz,upky->bcdxyz/dot_general | solution.py:99
  705.6 12.0 %copy.144 = f32[1,4,4,8,128,128]{5,2,1,4,3,0:T(4,128)} copy(f32[1,4,4,8,128,128]{5,4,3,2,1,0:T(8,128)} %fusion.46) | data formatting | bytes 16777216 | tf_op jit(solution)/shard_map/bcdxpkuz,upky->bcdxyz/transpose | solution.py:99
  717.6 12.1 %fusion.17 = f32[1,16,8,128,128]{4,1,3,2,0:T(8,128)S(1)} fusion(f32[16,8,128,128]{3,0,2,1:T(8,128)} %bitcast.392, f32[1,16,8,128,128]{4,1,3,2,0:T(8,128)} %copy-done.1, f32[16,16]{1,0:T(8,128)S(1)} %copy-done), kind=kOutput, calls=%fused_computation.24 | convolution fusion | flops 404750336 | bytes 25166848 | tf_op jit(solution)/shard_map/boxyz,io->bixyz/dot_general | solution.py:161
  729.7 6.0 copy.146
  (94 shorter events, 5.1 us)
Async XLA Ops:
  0.6 343.6 %copy-start = (f32[16,16]{1,0:T(8,128)S(1)}, f32[16,16]{1,0:T(8,128)}, u32[]{:S(2)}) copy-start(f32[16,16]{1,0:T(8,128)} %param.8) | copy-start | bytes 3076
  1.1 10.2 %copy-start.19 = (f32[128,1,4,16]{0,3,2,1:T(8,128)}, f32[128,1,4,16]{0,3,2,1:T(8,128)S(1)}, u32[]{:S(2)}) copy-start(f32[128,1,4,16]{0,3,2,1:T(8,128)S(1)} %get-tuple-element.49) | copy-start | bytes 98308
  1.1 10.2 %copy-start.20 = (f32[128,1,4,16]{0,3,2,1:T(8,128)}, f32[128,1,4,16]{0,3,2,1:T(8,128)S(1)}, u32[]{:S(2)}) copy-start(f32[128,1,4,16]{0,3,2,1:T(8,128)S(1)} %get-tuple-element.50) | copy-start | bytes 98308
  11.3 7.1 copy-start.11
  11.3 7.1 copy-start.13
  38.8 56.8 %all-to-all-start = ((f32[1,16,16,8,256]{4,3,2,0,1:T(8,128)}), f32[1,16,16,8,256]{4,3,2,0,1:T(8,128)S(1)}, u32[]{:S(2)}, u32[]{:S(2)}) async-start(f32[1,16,16,8,256]{4,3,2,0,1:T(8,128)} %bitcast.51), calls=%async_computation | async-start | bytes 4194304 | tf_op jit(solution)/shard_map/all_to_all | solution.py:53
  95.7 1.3 copy-start.2
  145.9 29.5 %all-to-all-start.1 = ((f32[4,1,65536]{2,1,0:T(1,128)}), f32[4,1,65536]{2,1,0:T(1,128)S(1)}, u32[]{:S(2)}, u32[]{:S(2)}) async-start(f32[4,1,65536]{2,1,0:T(1,128)} %reshape.821), calls=%async_computation.1 | async-start | bytes 2097152 | tf_op jit(solution)/shard_map/all_to_all | solution.py:62
  204.8 7.5 %copy-start.3 = (f32[16,512,16]{1,0,2:T(8,128)}, f32[16,512,16]{1,0,2:T(8,128)S(1)}, u32[]{:S(2)}) copy-start(f32[16,512,16]{1,0,2:T(8,128)S(1)} %get-tuple-element.35) | copy-start | bytes 1572868
  204.8 7.5 %copy-start.5 = (f32[16,512,16]{1,0,2:T(8,128)}, f32[16,512,16]{1,0,2:T(8,128)S(1)}, u32[]{:S(2)}) copy-start(f32[16,512,16]{1,0,2:T(8,128)S(1)} %get-tuple-element.36) | copy-start | bytes 1572868
  213.6 28.7 %all-to-all-start.2 = ((f32[1,16,16,2,512]{4,1,3,0,2:T(8,128)}), f32[1,16,16,2,512]{4,1,3,0,2:T(8,128)S(1)}, u32[]{:S(2)}, u32[]{:S(2)}) async-start(f32[1,16,16,2,512]{4,1,3,0,2:T(8,128)} %pad_maximum_fusion.1), calls=%async_computation.2 | async-start | bytes 2097152 | tf_op jit(solution)/shard_map/all_to_all | solution.py:71
  217.3 37.6 %copy-start.7 = (f32[1,64,128,2]{2,1,0,3:T(8,128)}, f32[1,64,128,2]{2,1,0,3:T(8,128)S(1)}, u32[]{:S(2)}) copy-start(f32[1,64,128,2]{2,1,0,3:T(8,128)S(1)} %get-tuple-element.37) | copy-start | bytes 196612
  217.3 37.6 %copy-start.9 = (f32[1,64,128,2]{2,1,0,3:T(8,128)}, f32[1,64,128,2]{2,1,0,3:T(8,128)S(1)}, u32[]{:S(2)}) copy-start(f32[1,64,128,2]{2,1,0,3:T(8,128)S(1)} %get-tuple-element.38) | copy-start | bytes 196612
  256.9 54.3 %all-to-all-start.3 = ((f32[1,1,16,128,256]{4,2,1,0,3:T(8,128)}), f32[1,1,16,128,256]{4,2,1,0,3:T(8,128)}, u32[]{:S(2)}, u32[]{:S(2)}) async-start(f32[1,1,16,128,256]{4,2,1,0,3:T(8,128)} %copy.116), calls=%async_computation.3 | async-start | bytes 4194304 | tf_op jit(solution)/shard_map/all_to_all | solution.py:81
  261.9 74.4 %copy-start.15 = (f32[1,32,2,128]{3,1,0,2:T(8,128)}, f32[1,32,2,128]{3,1,0,2:T(8,128)S(1)}, u32[]{:S(2)}) copy-start(f32[1,32,2,128]{3,1,0,2:T(8,128)S(1)} %get-tuple-element.41) | copy-start | bytes 98308
  262.0 74.4 %copy-start.17 = (f32[1,32,2,128]{3,1,0,2:T(8,128)}, f32[1,32,2,128]{3,1,0,2:T(8,128)S(1)}, u32[]{:S(2)}) copy-start(f32[1,32,2,128]{3,1,0,2:T(8,128)S(1)} %get-tuple-element.42) | copy-start | bytes 98308
  322.3 14.2 %copy-start.21 = (f32[1,4,16,128]{3,2,0,1:T(8,128)S(1)}, f32[1,4,16,128]{3,2,0,1:T(8,128)}, u32[]{:S(2)}) copy-start(f32[1,4,16,128]{3,2,0,1:T(8,128)} %get-tuple-element.45) | copy-start | bytes 98308
  322.3 14.2 %copy-start.23 = (f32[1,4,16,128]{3,2,0,1:T(8,128)S(1)}, f32[1,4,16,128]{3,2,0,1:T(8,128)}, u32[]{:S(2)}) copy-start(f32[1,4,16,128]{3,2,0,1:T(8,128)} %get-tuple-element.46) | copy-start | bytes 98308
  322.3 22.0 %slice-start = ((s8[8388608]{0:T(1024)(128)(4,1)}), s8[4194304]{0:T(1024)(128)(4,1)S(1)}, s32[]{:S(2)}) async-start(s8[8388608]{0:T(1024)(128)(4,1)} %bitcast.394), calls=%async_computation.8 | async-start | bytes 8388608
  322.3 22.0 %slice-start.4 = ((s8[8388608]{0:T(1024)(128)(4,1)}), s8[4194304]{0:T(1024)(128)(4,1)S(1)}, s32[]{:S(2)}) async-start(s8[8388608]{0:T(1024)(128)(4,1)} %bitcast.407), calls=%async_computation.12 | async-start | bytes 8388608
  336.4 7.8 %slice-start.1 = ((s8[8388608]{0:T(1024)(128)(4,1)}), s8[4194304]{0:T(1024)(128)(4,1)S(1)}, s32[]{:S(2)}) async-start(s8[8388608]{0:T(1024)(128)(4,1)} %bitcast.394), calls=%async_computation.9 | async-start | bytes 8388608
  336.4 7.8 %slice-start.5 = ((s8[8388608]{0:T(1024)(128)(4,1)}), s8[4194304]{0:T(1024)(128)(4,1)S(1)}, s32[]{:S(2)}) async-start(s8[8388608]{0:T(1024)(128)(4,1)} %bitcast.407), calls=%async_computation.13 | async-start | bytes 8388608
  336.4 7.8 %copy-start.25 = (f32[16]{0:T(128)S(1)}, f32[16]{0:T(128)}, u32[]{:S(2)}) copy-start(f32[16]{0:T(128)} %param.9) | copy-start | bytes 196
  366.3 11.7 %copy-start.1 = (f32[1,16,8,128,128]{4,1,3,2,0:T(8,128)}, f32[1,16,8,128,128]{4,1,3,2,0:T(8,128)S(1)}, u32[]{:S(2)}) copy-start(f32[1,16,8,128,128]{4,1,3,2,0:T(8,128)S(1)} %get-tuple-element.57) | copy-start | bytes 25165828
  366.3 11.7 %copy-start.12 = (f32[1,128,2,32]{1,3,0,2:T(8,128)S(1)}, f32[1,128,2,32]{1,3,0,2:T(8,128)}, u32[]{:S(2)}) copy-start(f32[1,128,2,32]{1,3,0,2:T(8,128)} %copy-done.11) | copy-start | bytes 98308
  366.3 11.7 %copy-start.14 = (f32[1,128,2,32]{1,3,0,2:T(8,128)S(1)}, f32[1,128,2,32]{1,3,0,2:T(8,128)}, u32[]{:S(2)}) copy-start(f32[1,128,2,32]{1,3,0,2:T(8,128)} %copy-done.13) | copy-start | bytes 98308
  550.4 10.8 %copy-start.4 = (f32[16,512,16]{1,0,2:T(8,128)S(1)}, f32[16,512,16]{1,0,2:T(8,128)}, u32[]{:S(2)}) copy-start(f32[16,512,16]{1,0,2:T(8,128)} %copy-done.3) | copy-start | bytes 1572868
  550.4 10.8 %copy-start.6 = (f32[16,512,16]{1,0,2:T(8,128)S(1)}, f32[16,512,16]{1,0,2:T(8,128)}, u32[]{:S(2)}) copy-start(f32[16,512,16]{1,0,2:T(8,128)} %copy-done.5) | copy-start | bytes 1572868
  573.9 31.4 %copy-start.8 = (f32[1,64,128,2]{2,1,0,3:T(8,128)S(1)}, f32[1,64,128,2]{2,1,0,3:T(8,128)}, u32[]{:S(2)}) copy-start(f32[1,64,128,2]{2,1,0,3:T(8,128)} %copy-done.7) | copy-start | bytes 196612
  573.9 31.4 %copy-start.10 = (f32[1,64,128,2]{2,1,0,3:T(8,128)S(1)}, f32[1,64,128,2]{2,1,0,3:T(8,128)}, u32[]{:S(2)}) copy-start(f32[1,64,128,2]{2,1,0,3:T(8,128)} %copy-done.9) | copy-start | bytes 196612
  616.6 54.1 %all-to-all-start.7 = ((f32[1,1,16,128,256]{4,2,1,0,3:T(8,128)}), f32[1,1,16,128,256]{4,2,1,0,3:T(8,128)}, u32[]{:S(2)}, u32[]{:S(2)}) async-start(f32[1,1,16,128,256]{4,2,1,0,3:T(8,128)} %copy.139), calls=%async_computation.7 | async-start | bytes 4194304 | tf_op jit(solution)/shard_map/all_to_all | solution.py:81
  621.2 11.0 %slice-start.2 = ((s8[8388608]{0:T(1024)(128)(4,1)}), s8[4194304]{0:T(1024)(128)(4,1)S(1)}, s32[]{:S(2)}) async-start(s8[8388608]{0:T(1024)(128)(4,1)} %bitcast.398), calls=%async_computation.10 | async-start | bytes 8388608
  626.2 6.0 slice-start.3
  642.8 38.9 %copy-start.16 = (f32[1,32,2,128]{3,1,0,2:T(8,128)S(1)}, f32[1,32,2,128]{3,1,0,2:T(8,128)}, u32[]{:S(2)}) copy-start(f32[1,32,2,128]{3,1,0,2:T(8,128)} %copy-done.15) | copy-start | bytes 98308
  642.8 38.9 %copy-start.18 = (f32[1,32,2,128]{3,1,0,2:T(8,128)S(1)}, f32[1,32,2,128]{3,1,0,2:T(8,128)}, u32[]{:S(2)}) copy-start(f32[1,32,2,128]{3,1,0,2:T(8,128)} %copy-done.17) | copy-start | bytes 98308
  681.7 13.8 %copy-start.22 = (f32[1,4,16,128]{3,2,0,1:T(8,128)S(1)}, f32[1,4,16,128]{3,2,0,1:T(8,128)}, u32[]{:S(2)}) copy-start(f32[1,4,16,128]{3,2,0,1:T(8,128)} %get-tuple-element.45) | copy-start | bytes 98308
  681.7 13.8 %copy-start.24 = (f32[1,4,16,128]{3,2,0,1:T(8,128)S(1)}, f32[1,4,16,128]{3,2,0,1:T(8,128)}, u32[]{:S(2)}) copy-start(f32[1,4,16,128]{3,2,0,1:T(8,128)} %get-tuple-element.46) | copy-start | bytes 98308
where the time goes:
time: 744 us; the launch traced here: 736 us
  local copies, waits for them, and re-layouts  238 us (32%)
  waiting for transfers between devices  176 us (24%)
  matrix products  141 us (19%)
  blocking collectives  109 us (15%)
  other arithmetic  46.7 us (6%)
  starting transfers between devices  24.1 us (3%)
    all_to_all x2, waiting for transfers between devices, synthesis(): lax.all_to_all(first_pass[:, None], ('planes', 'chan'), split_axis=3, con...  76.2 us
    unnamed x71, local copies, waits for them, and re-layouts  68.4 us
    another operation x8, local copies, waits for them, and re-layouts  58.7 us
    all_to_all x1, blocking collectives, analysis(): lax.all_to_all(spectra, ('planes', 'chan'), split_axis=1, concat_axis=3,...  52.5 us
    all_to_all x1, waiting for transfers between devices, analysis(): lax.all_to_all(spectra, ('planes', 'chan'), split_axis=1, concat_axis=3,...  49.2 us
    all_to_all x1, blocking collectives, analysis(): lax.all_to_all(first_pass, 'chan', split_axis=4, concat_axis=2, tiled=True)  28.7 us
    dot_general x2, matrix products, synthesis(): jnp.einsum(source_form + ',tmuz->bcdxpkuz', returned, third_inverse, prec...  27.9 us
    all_to_all x1, blocking collectives, synthesis(): lax.all_to_all(spectrum, 'chan', split_axis=2, concat_axis=4, tiled=True)  27.7 us
  transfers between devices with their start and end apart: 5, of which 5 were waited for; matrix products, arithmetic and copies ran while one was open for 3% of the time, Pallas kernels for 0%

commit v1 on v0

v1 whole, which is shorter than its diff:
```python
import functools
import math

import jax
import jax.numpy as jnp
import numpy as np
from jax import lax
from jax.experimental import pallas as pl
from jax.experimental.pallas import tpu as pltpu
from jax.sharding import PartitionSpec as P

HIGH = lax.Precision.HIGH
F32 = jnp.float32
GRANT = 56 * 1024 * 1024


def dot(a, b):
    return jnp.dot(a, b, precision=HIGH, preferred_element_type=F32)


def angles(length, freqs):
    turns = np.outer(np.arange(length), freqs) % length
    return turns * (2.0 * math.pi / length)


def retained(length, modes):
    index = np.arange(2 * modes)
    return np.where(index < modes, index, length - 2 * modes + index)


class Tables:
    def __init__(self, gx, gy, gz, modes, width):
        ay = angles(gy, retained(gy, modes))
        self.y = np.concatenate([np.cos(ay).T, np.sin(ay).T], 0).astype(np.float32)
        self.y_inv = np.concatenate([np.cos(ay), np.sin(ay)], 1).astype(np.float32)
        az = angles(gz, np.arange(modes))
        cz, sz = np.cos(az), np.sin(az)
        z = np.zeros((width, 2, gz, 2, width, modes))
        z_inv = np.zeros((2, width, modes, width, 2, gz))
        for d in range(width):
            z[d, 0, :, 0, d] = cz
            z[d, 1, :, 0, d] = -sz
            z[d, 0, :, 1, d] = -sz
            z[d, 1, :, 1, d] = -cz
            z_inv[0, d, :, d, 0] = cz.T
            z_inv[1, d, :, d, 0] = -sz.T
            z_inv[0, d, :, d, 1] = -sz.T
            z_inv[1, d, :, d, 1] = -cz.T
        self.z = z.reshape(width * 2 * gz, 2 * width * modes).astype(np.float32)
        self.z_inv = z_inv.reshape(2 * width * modes, width * 2 * gz).astype(np.float32)
        ax = angles(gx, retained(gx, modes))
        self.x = np.concatenate([np.cos(ax).T, np.sin(ax).T], 0).astype(np.float32)
        self.x_inv = np.concatenate([np.cos(ax), np.sin(ax)], 1).astype(np.float32)


def analysis_rows(planes, y_table, z_table, channels, groups):
    second = dot(y_table, planes)
    rows = second.shape[0] // 2
    gz = planes.shape[1] // channels
    width = channels // groups
    stacked = []
    for c in range(groups):
        parts = []
        for d in range(width):
            lanes = slice((c * width + d) * gz, (c * width + d + 1) * gz)
            parts.append(second[:rows, lanes])
            parts.append(second[rows:, lanes])
        stacked.append(jnp.concatenate(parts, 1))
    return dot(jnp.concatenate(stacked, 0), z_table)


class Exchange:
    def __init__(self, plane_count, groups):
        self.groups = groups
        self.count = plane_count * groups
        self.plane = lax.axis_index("planes")
        self.chan = lax.axis_index("chan")
        self.me = self.plane * groups + self.chan

    def barrier(self):
        semaphore = pltpu.get_barrier_semaphore()

        def greet(offset, carry):
            other = lax.rem(self.me + offset, self.count)
            pl.semaphore_signal(
                semaphore,
                inc=1,
                device_id={"planes": other // self.groups, "chan": lax.rem(other, self.groups)},
                device_id_type=pl.DeviceIdType.MESH,
            )
            return carry

        lax.fori_loop(1, self.count, greet, 0)
        pl.semaphore_wait(semaphore, self.count - 1)

    def to_all(self, source, target, local_planes, x, send, recv):
        def one(offset, carry):
            other = lax.rem(self.me + offset, self.count)
            pltpu.make_async_remote_copy(
                src_ref=source.at[other * local_planes + x],
                dst_ref=target.at[self.me * local_planes + x],
                send_sem=send,
                recv_sem=recv,
                device_id={"planes": other // self.groups, "chan": lax.rem(other, self.groups)},
                device_id_type=pl.DeviceIdType.MESH,
            ).start()
            return carry

        lax.fori_loop(1, self.count, one, 0)

    def to_chan(self, source, target, send, recv):
        def one(offset, carry):
            other = lax.rem(self.chan + offset, self.groups)
            pltpu.make_async_remote_copy(
                src_ref=source(other),
                dst_ref=target(self.chan),
                send_sem=send,
                recv_sem=recv,
                device_id={"chan": other},
                device_id_type=pl.DeviceIdType.MESH,
            ).start()
            return carry

        lax.fori_loop(1, self.groups, one, 0)


def drain(ref, semaphore):
    pltpu.make_async_copy(ref, ref, semaphore).wait()


def send_plane(net, result, x, local_planes, kl, send, recv, sems):
    rows = net.count // net.groups * kl
    for c in range(net.groups):
        for p in range(net.count // net.groups):
            start = c * rows + p * kl
            send[(p * net.groups + c) * local_planes + x] = result[start : start + kl]
    mine = net.me * local_planes + x
    recv[mine] = send[mine]
    net.to_all(send, recv, local_planes, x, sems.at[0], sems.at[1])


def finish_analysis(net, table_ref, out_ref, send, recv, blocks, sems, local_planes):
    others = (net.count - 1) * local_planes
    drain(recv.at[pl.ds(0, others)], sems.at[1])
    table = table_ref[...]
    groups, kl, fl, lanes = blocks.shape
    half = lanes // 2
    rows = groups * fl
    for k in range(kl):
        both = dot(table, recv[:, k, :])
        cosine, sine = both[:rows], both[rows:]
        re = cosine[:, :half] + sine[:, half:]
        im = cosine[:, half:] - sine[:, :half]
        value = jnp.concatenate([re, im], 1)
        for c in range(groups):
            blocks[c, k] = value[c * fl : (c + 1) * fl]
        net.to_chan(
            lambda c: blocks.at[c, k], lambda c: out_ref.at[c, k], sems.at[2], sems.at[3]
        )
    own = pltpu.make_async_copy(blocks.at[net.chan], out_ref.at[net.chan], sems.at[4])
    own.start()
    own.wait()
    drain(send.at[pl.ds(0, others)], sems.at[0])
    drain(blocks.at[pl.ds(0, groups - 1)], sems.at[2])
    drain(out_ref.at[pl.ds(0, groups - 1)], sems.at[3])


def start_synthesis(net, in_ref, table_ref, blocks, send, recv, sems, plane_sems, local_planes):
    net.to_chan(
        lambda c: in_ref.at[c], lambda c: blocks.at[c], sems.at[0], sems.at[1]
    )
    own = pltpu.make_async_copy(in_ref.at[net.chan], blocks.at[net.chan], sems.at[2])
    own.start()
    own.wait()
    groups, kl, _, lanes = blocks.shape
    drain(blocks.at[pl.ds(0, groups - 1)], sems.at[1])
    table = table_ref[...]
    half = lanes // 2
    for k in range(kl):
        value = jnp.concatenate([blocks[c, k] for c in range(groups)], 0)
        turned = jnp.concatenate([-value[:, half:], value[:, :half]], 1)
        send[:, k, :] = dot(table, jnp.concatenate([value, turned], 0))
    mine = pl.ds(net.me * local_planes, local_planes)
    recv[mine] = send[mine]

    def plane(x, carry):
        net.to_all(send, recv, local_planes, x, sems.at[3], plane_sems.at[x])
        return carry

    lax.fori_loop(0, local_planes, plane, 0)


def finish_synthesis(net, in_ref, send, sems, local_planes):
    drain(in_ref.at[pl.ds(0, net.groups - 1)], sems.at[0])
    drain(send.at[pl.ds(0, (net.count - 1) * local_planes)], sems.at[3])


def synthesis_planes(net, recv, x, local_planes, y_inv, z_inv, channels):
    width = channels // net.groups
    gz = z_inv.shape[1] // (2 * width)
    kl = recv.shape[1]
    plane_count = net.count // net.groups
    rows = plane_count * kl
    stacked = [
        recv[(p * net.groups + c) * local_planes + x]
        for c in range(net.groups)
        for p in range(plane_count)
    ]
    depth = dot(jnp.concatenate(stacked, 0), z_inv)
    parts = []
    for c in range(net.groups):
        block = depth[c * rows : (c + 1) * rows]
        for d in range(width):
            base = 2 * d * gz
            parts.append(
                jnp.concatenate(
                    [block[:, base : base + gz], block[:, base + gz : base + 2 * gz]], 0
                )
            )
    return dot(y_inv, jnp.concatenate(parts, 1))


def first_kernel(
    plane_count, groups, field_ref, y_ref, z_ref, x_ref, out_ref, send, recv, blocks, sems
):
    net = Exchange(plane_count, groups)
    x, local_planes = pl.program_id(0), recv.shape[0] // net.count
    pl.when(x == 0)(net.barrier)
    channels = field_ref.shape[1]
    planes = jnp.concatenate([field_ref[0, i, 0] for i in range(channels)], 1)
    result = analysis_rows(planes, y_ref[...], z_ref[...], channels, groups)
    send_plane(net, result, x, local_planes, recv.shape[1], send, recv, sems)

    @pl.when(x == local_planes - 1)
    def _():
        finish_analysis(net, x_ref, out_ref, send, recv, blocks, sems, local_planes)


def middle_kernel(
    plane_count,
    groups,
    weight_ref,
    bias_ref,
    in_ref,
    field_ref,
    cot_ref,
    y_inv_ref,
    z_inv_ref,
    x_inv_ref,
    y_ref,
    z_ref,
    x_ref,
    out_ref,
    grad_ref,
    next_ref,
    spectral,
    pre_grad,
    back_blocks,
    back_send,
    back_recv,
    back_sems,
    plane_sems,
    send,
    recv,
    blocks,
    sems,
):
    net = Exchange(plane_count, groups)
    x, local_planes = pl.program_id(0), recv.shape[0] // net.count
    channels, gy, gz = field_ref.shape[1], field_ref.shape[3], field_ref.shape[4]

    @pl.when(x == 0)
    def _():
        net.barrier()
        start_synthesis(
            net,
            in_ref,
            x_inv_ref,
            back_blocks,
            back_send,
            back_recv,
            back_sems,
            plane_sems,
            local_planes,
        )

    drain(back_recv.at[pl.ds(0, net.count - 1)], plane_sems.at[x])
    spectral[...] = synthesis_planes(
        net, back_recv, x, local_planes, y_inv_ref[...], z_inv_ref[...], channels
    )
    step = 16

    def chunk(j, carry):
        rows = pl.ds(pl.multiple_of(j * step, step), step)
        inputs = [field_ref[0, i, 0, rows, :] for i in range(channels)]
        grads = []
        for o in range(channels):
            lanes = slice(o * gz, (o + 1) * gz)
            pre = spectral[rows, lanes] + bias_ref[o]
            for i in range(channels):
                pre = pre + inputs[i] * weight_ref[i, o]
            cdf = 0.5 * (1.0 + lax.erf(pre * (1.0 / math.sqrt(2.0))))
            out_ref[0, o, 0, rows, :] = pre * cdf
            slope = cdf + pre * jnp.exp(-0.5 * pre * pre) * (1.0 / math.sqrt(2.0 * math.pi))
            grad = cot_ref[0, o, 0, rows, :] * slope
            pre_grad[rows, lanes] = grad
            grads.append(grad)
        for i in range(channels):
            total = grads[0] * weight_ref[i, 0]
            for o in range(1, channels):
                total = total + grads[o] * weight_ref[i, o]
            grad_ref[0, i, 0, rows, :] = total
        return carry

    lax.fori_loop(0, gy // step, chunk, 0)
    result = analysis_rows(pre_grad[...], y_ref[...], z_ref[...], channels, groups)
    send_plane(net, result, x, local_planes, recv.shape[1], send, recv, sems)

    @pl.when(x == local_planes - 1)
    def _():
        finish_analysis(net, x_ref, next_ref, send, recv, blocks, sems, local_planes)
        finish_synthesis(net, in_ref, back_send, back_sems, local_planes)


def last_kernel(
    plane_count,
    groups,
    in_ref,
    grad_ref,
    y_inv_ref,
    z_inv_ref,
    x_inv_ref,
    out_ref,
    blocks,
    send,
    recv,
    sems,
    plane_sems,
):
    net = Exchange(plane_count, groups)
    x, local_planes = pl.program_id(0), recv.shape[0] // net.count
    channels, gz = grad_ref.shape[1], grad_ref.shape[4]

    @pl.when(x == 0)
    def _():
        net.barrier()
        start_synthesis(
            net, in_ref, x_inv_ref, blocks, send, recv, sems, plane_sems, local_planes
        )

    drain(recv.at[pl.ds(0, net.count - 1)], plane_sems.at[x])
    planes = synthesis_planes(
        net, recv, x, local_planes, y_inv_ref[...], z_inv_ref[...], channels
    )
    for i in range(channels):
        out_ref[0, i, 0] = grad_ref[0, i, 0] + planes[:, i * gz : (i + 1) * gz]

    @pl.when(x == local_planes - 1)
    def _():
        finish_synthesis(net, in_ref, send, sems, local_planes)


def mix_kernel(spec_ref, weight_ref, scale_ref, out_ref):
    channels = spec_ref.shape[1]
    scale = scale_ref[...]

    def one(o, carry):
        re = jnp.zeros(spec_ref.shape[2:], F32)
        im = re
        for i in range(channels):
            wr, wi = weight_ref[0, i, o], weight_ref[1, i, o]
            sr, si = spec_ref[0, i], spec_ref[1, i]
            re = re + (sr * wr - si * wi)
            im = im + (sr * wi + si * wr)
        out_ref[0, o] = re * scale
        out_ref[1, o] = im * scale
        return carry

    lax.fori_loop(0, weight_ref.shape[2], one, 0)


def back_kernel(grad_ref, weight_ref, scale_ref, out_ref):
    channels = grad_ref.shape[1]
    scale = scale_ref[...]

    def one(i, carry):
        re = jnp.zeros(grad_ref.shape[2:], F32)
        im = re
        for o in range(channels):
            wr, wi = weight_ref[0, i, o], weight_ref[1, i, o]
            gr, gi = grad_ref[0, o], grad_ref[1, o]
            re = re + (gr * wr + gi * wi)
            im = im + (gi * wr - gr * wi)
        out_ref[0, i] = re * scale
        out_ref[1, i] = im * scale
        return carry

    lax.fori_loop(0, weight_ref.shape[1], one, 0)


def outer_kernel(spec_ref, grad_ref, scale_ref, out_ref):
    channels = spec_ref.shape[1]
    scale = scale_ref[...]

    def one(i, carry):
        sr, si = spec_ref[0, i] * scale, spec_ref[1, i] * scale
        for o in range(channels):
            gr, gi = grad_ref[0, o], grad_ref[1, o]
            out_ref[0, i, o] = sr * gr + si * gi
            out_ref[1, i, o] = sr * gi - si * gr
        return carry

    lax.fori_loop(0, channels, one, 0)


def params(collective_id=None):
    if collective_id is None:
        return pltpu.CompilerParams(vmem_limit_bytes=GRANT)
    return pltpu.CompilerParams(
        vmem_limit_bytes=GRANT, collective_id=collective_id, has_side_effects=True
    )


def whole(array):
    return pl.BlockSpec(array.shape, lambda *_: (0,) * array.ndim)


def planes_spec(shape):
    return pl.BlockSpec((1, shape[1], 1, shape[3], shape[4]), lambda x: (0, 0, x, 0, 0))


def modes_spec(shape):
    tile = min(128, shape[-1])
    lead = len(shape) - 1
    return pl.BlockSpec(shape[:-1] + (tile,), lambda n: (0,) * lead + (n,))


def shape_of(dims):
    return jax.ShapeDtypeStruct(dims, F32)


def local(plane_count, groups, field, cotangent, spec_weight, point_weight, bias):
    _, channels, local_planes, gy, gz = field.shape
    gx = local_planes * plane_count * groups
    kl = spec_weight.shape[3]
    modes = kl * plane_count // 2
    fl = spec_weight.shape[4] // modes
    width = channels // groups
    lanes = 2 * width * modes
    tables = Tables(gx, gy, gz, modes, width)
    y, z, x = jnp.asarray(tables.y), jnp.asarray(tables.z), jnp.asarray(tables.x)
    y_inv, z_inv, x_inv = (
        jnp.asarray(tables.y_inv),
        jnp.asarray(tables.z_inv),
        jnp.asarray(tables.x_inv),
    )
    weighting = np.where(np.arange(fl * modes) % modes == 0, 1.0, 2.0) / float(gx * gy * gz)
    scale = jnp.asarray(weighting.astype(np.float32)[None, :])
    block_shape = (groups, kl, fl, lanes)
    mode_shape = (2, channels, kl, fl * modes)
    plane_rows = pltpu.VMEM((gx, kl, lanes), F32)
    mode_rows = pltpu.VMEM(block_shape, F32)
    semaphores = pltpu.SemaphoreType.DMA((5,))
    plane_semaphores = pltpu.SemaphoreType.DMA((local_planes,))
    anywhere = pl.BlockSpec(memory_space=pl.ANY)
    smem = pl.BlockSpec(memory_space=pltpu.SMEM)
    plane_block = planes_spec(field.shape)

    def to_modes(blocks):
        blocks = blocks.reshape(groups, kl, fl, 2, width, modes)
        return blocks.transpose(3, 0, 4, 1, 2, 5).reshape(mode_shape)

    def from_modes(mixed):
        blocks = mixed.reshape(2, groups, width, kl, fl, modes).transpose(1, 3, 4, 0, 2, 5)
        return blocks.reshape(block_shape)

    blocks = pl.pallas_call(
        functools.partial(first_kernel, plane_count, groups),
        grid=(local_planes,),
        in_specs=[plane_block, whole(y), whole(z), whole(x)],
        out_specs=anywhere,
        out_shape=shape_of(block_shape),
        scratch_shapes=[plane_rows, plane_rows, mode_rows, semaphores],
        compiler_params=params(1),
        name="first",
    )(field, y, z, x)
    spectrum = to_modes(blocks)
    mode_block = modes_spec(mode_shape)
    weight_block = modes_spec(spec_weight.shape)
    scale_block = modes_spec(scale.shape)
    mode_grid = (mode_shape[-1] // min(128, mode_shape[-1]),)
    mixed = pl.pallas_call(
        mix_kernel,
        grid=mode_grid,
        in_specs=[mode_block, weight_block, scale_block],
        out_specs=mode_block,
        out_shape=shape_of(mode_shape),
        compiler_params=params(),
        name="mix",
    )(spectrum, spec_weight, scale)
    output, local_grad, blocks = pl.pallas_call(
        functools.partial(middle_kernel, plane_count, groups),
        grid=(local_planes,),
        in_specs=[smem, smem, anywhere, plane_block, plane_block]
        + [whole(y_inv), whole(z_inv), whole(x_inv), whole(y), whole(z), whole(x)],
        out_specs=[plane_block, plane_block, anywhere],
        out_shape=[shape_of(field.shape), shape_of(field.shape), shape_of(block_shape)],
        scratch_shapes=[pltpu.VMEM((gy, channels * gz), F32)] * 2
        + [mode_rows, plane_rows, plane_rows, semaphores, plane_semaphores]
        + [plane_rows, plane_rows, mode_rows, semaphores],
        compiler_params=params(2),
        name="middle",
    )(
        point_weight,
        bias,
        from_modes(mixed),
        field,
        cotangent,
        y_inv,
        z_inv,
        x_inv,
        y,
        z,
        x,
    )
    grad_modes = to_modes(blocks)
    spectrum_grad = pl.pallas_call(
        back_kernel,
        grid=mode_grid,
        in_specs=[mode_block, weight_block, scale_block],
        out_specs=mode_block,
        out_shape=shape_of(mode_shape),
        compiler_params=params(),
        name="back",
    )(grad_modes, spec_weight, scale)
    weight_grad = pl.pallas_call(
        outer_kernel,
        grid=mode_grid,
        in_specs=[mode_block, mode_block, scale_block],
        out_specs=weight_block,
        out_shape=shape_of(spec_weight.shape),
        compiler_params=params(),
        name="weight_grad",
    )(spectrum, grad_modes, scale)
    field_grad = pl.pallas_call(
        functools.partial(last_kernel, plane_count, groups),
        grid=(local_planes,),
        in_specs=[anywhere, plane_block, whole(y_inv), whole(z_inv), whole(x_inv)],
        out_specs=plane_block,
        out_shape=shape_of(field.shape),
        scratch_shapes=[mode_rows, plane_rows, plane_rows, semaphores, plane_semaphores],
        compiler_params=params(3),
        name="last",
    )(from_modes(spectrum_grad), local_grad, y_inv, z_inv, x_inv)
    return (output, field_grad, weight_grad)


def solution(mesh):
    shard = P("groups", None, ("planes", "chan"), None, None)
    in_specs = (shard, shard, P(None, None, None, "planes", "chan"), P(), P())
    out_specs = (shard, shard, P("groups", None, None, "planes", "chan"))
    function = functools.partial(local, mesh.shape["planes"], mesh.shape["chan"])
    return jax.shard_map(
        function, mesh=mesh, in_specs=in_specs, out_specs=out_specs, check_vma=False
    )
```

time: 744 us -> 399 us (0.54); the launches traced: 736 us -> 398 us
  Pallas kernels: 0 us -> 328 us
  waiting for transfers between devices: 176 us -> 0 us
  local copies, waits for them, and re-layouts: 238 us -> 70 us
  matrix products: 141 us -> 0 us
  blocking collectives: 109 us -> 0 us
  other arithmetic: 46.7 us -> 0 us
  starting transfers between devices: 24.1 us -> 0 us
    pallas_call x0 -> x6, Pallas kernels: none -> 328 us  [the longest x1 146 us: local(): pl.pallas_call(functools.partial(middle_kernel, plane_count, groups), gri...]
    all_to_all x5 -> x0, waiting for transfers between devices: 176 us -> none  [the longest x2 76.2 us: synthesis(): lax.all_to_all(first_pass[:, None], ('planes', 'chan'), split_axis=3, con...]
    dot_general x14 -> x0, matrix products: 141 us -> none  [the longest x2 27.9 us: synthesis(): jnp.einsum(source_form + ',tmuz->bcdxpkuz', returned, third_inverse, prec...]
    all_to_all x3 -> x0, blocking collectives: 109 us -> none  [the longest x1 52.5 us: analysis(): lax.all_to_all(spectra, ('planes', 'chan'), split_axis=1, concat_axis=3,...]
    another operation x10 -> x0, local copies, waits for them, and re-layouts: 62.7 us -> none
    unnamed x71 -> x4, local copies, waits for them, and re-layouts: 68.4 us -> 11.4 us
    all_to_all x11 -> x0, local copies, waits for them, and re-layouts: 30.8 us -> none  [the longest x5 21.8 us: analysis(): lax.all_to_all(first_pass, 'chan', split_axis=4, concat_axis=2, tiled=True)]
    transpose x5 -> x0, local copies, waits for them, and re-layouts: 28.3 us -> none  [the longest x2 15.9 us: analysis(): jnp.einsum('bcdxspkz,sztm->bpckxdtm', second_pass, third_table, precision...]
  transfers between devices with their start and end apart: 5 -> 0, of which waited for: 5 -> 0; matrix products, arithmetic and copies ran while one was open for 3% -> 0% of each run, Pallas kernels for 0% -> 0%
where the time goes in v1:
time: 399 us; the launch traced here: 398 us
  Pallas kernels  328 us (82%)
  local copies, waits for them, and re-layouts  70 us (18%)
    pallas_call x1, Pallas kernels, local(): pl.pallas_call(functools.partial(middle_kernel, plane_count, groups), gri...  146 us
    pallas_call x1, Pallas kernels, local(): pl.pallas_call(functools.partial(first_kernel, plane_count, groups), grid...  80 us
    pallas_call x1, Pallas kernels, local(): pl.pallas_call(functools.partial(last_kernel, plane_count, groups), grid=...  76.2 us
    reshape x4, local copies, waits for them, and re-layouts, from_modes(): mixed.reshape(2, groups, width, kl, fl, modes).transpose(1, 3, 4, 0, 2, 5)  21.3 us
    reshape x4, local copies, waits for them, and re-layouts, to_modes(): blocks = blocks.reshape(groups, kl, fl, 2, width, modes)  18.6 us
    unnamed x4, local copies, waits for them, and re-layouts  11.4 us
    reshape x2, local copies, waits for them, and re-layouts, from_modes(): return blocks.reshape(block_shape)  9.92 us
    pallas_call x1, Pallas kernels, local(): pl.pallas_call(mix_kernel, grid=mode_grid, in_specs=[mode_block, weight_b...  9.38 us

profile of v1, /device:TPU:0, one launch (start us, length us, event | category | flops | bytes accessed | tf_op | source)
XLA Modules:
  0.0 398.4 jit_solution(11323488795480356068)
XLA Ops:
  0.6 80.0 %first.1 = f32[4,16,16,256]{3,2,1,0:T(8,128)} custom-call(f32[1,16,8,128,128]{4,3,2,1,0:T(8,128)} %field_ref.3, f32[128,128]{1,0:T(8,128)} %constant.10.clone.y_ref.x_ref, f32[1024,256]{1,0:T(8,128)} %constant.11.clone.z_ref, f32[128,128]{1,0:T(8,128)} %constant.10.clone.y_ref.x_ref), custom_call_target="tpu_custom_call" | custom-call | tf_op jit(solution)/shard_map/first/pallas_call | solution.py:477
  80.6 4.3 %reshape.30 = f32[4,16,16,2,4,32]{5,4,3,2,1,0:T(4,128)} reshape(f32[4,16,16,256]{3,2,1,0:T(8,128)} %first.1) | data formatting | bytes 2097152 | tf_op jit(solution)/shard_map/reshape | solution.py:470
  84.9 5.0 %copy.26 = f32[4,16,16,2,4,32]{5,2,1,4,0,3:T(8,128)} copy(f32[4,16,16,2,4,32]{5,4,3,2,1,0:T(4,128)} %reshape.30) | data formatting | bytes 2097152 | tf_op jit(solution)/shard_map/reshape | solution.py:470
  90.0 4.4 %reshape.31.spec_ref = f32[2,16,16,512]{3,2,1,0:T(8,128)} reshape(f32[2,4,4,16,16,32]{5,4,3,2,1,0:T(8,128)} %bitcast.24) | data formatting | bytes 2097152 | tf_op jit(solution)/shard_map/reshape | solution.py:471
  94.3 9.4 %mix.1 = f32[2,16,16,512]{3,2,1,0:T(8,128)} custom-call(f32[2,16,16,512]{3,2,1,0:T(8,128)} %reshape.31.spec_ref, f32[2,16,16,16,512]{4,3,2,1,0:T(8,128)} %weight_ref.5, f32[1,512]{1,0:T(1,128)} %constant.14.clone.scale_ref), custom_call_target="tpu_custom_call" | custom-call | tf_op jit(solution)/shard_map/mix/pallas_call | solution.py:492
  103.7 3.7 reshape.32
  107.5 6.9 %copy.25 = f32[2,4,4,16,16,32]{5,2,0,4,3,1:T(4,128)} copy(f32[2,4,4,16,16,32]{5,4,3,2,1,0:T(8,128)} %reshape.32) | data formatting | bytes 2097152 | tf_op jit(solution)/shard_map/reshape | solution.py:474
  114.4 5.0 %reshape.33.in_ref = f32[4,16,16,256]{3,2,1,0:T(8,128)} reshape(f32[4,16,16,2,4,32]{5,4,3,2,1,0:T(4,128)} %bitcast.25) | data formatting | bytes 2097152 | tf_op jit(solution)/shard_map/reshape | solution.py:475
  119.3 145.8 %middle.1 = (f32[1,16,8,128,128]{4,3,2,1,0:T(8,128)}, f32[1,16,8,128,128]{4,3,2,1,0:T(8,128)}, f32[4,16,16,256]{3,2,1,0:T(8,128)}) custom-call(f32[16,16]{1,0:T(8,128)} %weight_ref.4, f32[16]{0:T(128)} %bias_ref.1, f32[4,16,16,256]{3,2,1,0:T(8,128)} %reshape.33.in_ref, f32[1,16,8,128,128]{4,3,2,1,0:T(8,128)} %field_ref.3, f32[1,16,8,128,128]{4,3,2,1,0:T(8,128)} %cot_ref.1, ...), custom_call_target="tpu_custom_call" | custom-call | tf_op jit(solution)/shard_map/middle/pallas_call | solution.py:501
  265.2 4.3 %reshape.34 = f32[4,16,16,2,4,32]{5,4,3,2,1,0:T(4,128)} reshape(f32[4,16,16,256]{3,2,1,0:T(8,128)} %get-tuple-element.7) | data formatting | bytes 2097152 | tf_op jit(solution)/shard_map/reshape | solution.py:470
  269.5 5.0 %copy.24 = f32[4,16,16,2,4,32]{5,2,1,4,0,3:T(8,128)} copy(f32[4,16,16,2,4,32]{5,4,3,2,1,0:T(4,128)} %reshape.34) | data formatting | bytes 2097152 | tf_op jit(solution)/shard_map/reshape | solution.py:470
  274.5 4.4 %reshape.35.grad_ref = f32[2,16,16,512]{3,2,1,0:T(8,128)} reshape(f32[2,4,4,16,16,32]{5,4,3,2,1,0:T(8,128)} %bitcast.26) | data formatting | bytes 2097152 | tf_op jit(solution)/shard_map/reshape | solution.py:471
  278.9 8.8 %back.1 = f32[2,16,16,512]{3,2,1,0:T(8,128)} custom-call(f32[2,16,16,512]{3,2,1,0:T(8,128)} %reshape.35.grad_ref, f32[2,16,16,16,512]{4,3,2,1,0:T(8,128)} %weight_ref.5, f32[1,512]{1,0:T(1,128)} %constant.14.clone.scale_ref), custom_call_target="tpu_custom_call" | custom-call | tf_op jit(solution)/shard_map/back/pallas_call | solution.py:527
  287.7 3.7 reshape.36
  291.4 6.9 %copy.23 = f32[2,4,4,16,16,32]{5,2,0,4,3,1:T(4,128)} copy(f32[2,4,4,16,16,32]{5,4,3,2,1,0:T(8,128)} %reshape.36) | data formatting | bytes 2097152 | tf_op jit(solution)/shard_map/reshape | solution.py:474
  298.3 5.0 %reshape.37.in_ref = f32[4,16,16,256]{3,2,1,0:T(8,128)} reshape(f32[4,16,16,2,4,32]{5,4,3,2,1,0:T(4,128)} %bitcast.27) | data formatting | bytes 2097152 | tf_op jit(solution)/shard_map/reshape | solution.py:475
  303.3 76.2 %last.1 = f32[1,16,8,128,128]{4,3,2,1,0:T(8,128)} custom-call(f32[4,16,16,256]{3,2,1,0:T(8,128)} %reshape.37.in_ref, f32[1,16,8,128,128]{4,3,2,1,0:T(8,128)} %get-tuple-element.8.grad_ref, f32[128,128]{1,0:T(8,128)} %constant.12.clone.y_inv_ref.x_inv_ref, f32[256,1024]{1,0:T(8,128)} %constant.13.clone.z_inv_ref, f32[128,128]{1,0:T(8,128)} %constant.12.clone.y_inv_ref.x_inv_ref), custom_call_target="tpu_custom_call" | custom-call | tf_op jit(solution)/shard_map/last/pallas_call | solution.py:545
  379.4 7.5 %weight_grad.1 = f32[2,16,16,16,512]{4,3,2,1,0:T(8,128)} custom-call(f32[2,16,16,512]{3,2,1,0:T(8,128)} %reshape.31.spec_ref, f32[2,16,16,512]{3,2,1,0:T(8,128)} %reshape.35.grad_ref, f32[1,512]{1,0:T(1,128)} %constant.14.clone.scale_ref), custom_call_target="tpu_custom_call" | custom-call | tf_op jit(solution)/shard_map/weight_grad/pallas_call | solution.py:536
  387.0 0.0 copy-start
  387.0 8.0 %copy.29 = f32[1,16,8,128,128]{4,3,2,1,0:T(8,128)} copy(f32[1,16,8,128,128]{4,3,2,1,0:T(8,128)} %get-tuple-element.12) | data formatting | bytes 16777216
  395.0 0.0 copy-done
  395.0 3.4 copy.30
Async XLA Ops:
  387.0 8.0 %copy-start = (f32[1,16,8,128,128]{4,3,2,1,0:T(8,128)S(1)}, f32[1,16,8,128,128]{4,3,2,1,0:T(8,128)}, u32[]{:S(2)}) copy-start(f32[1,16,8,128,128]{4,3,2,1,0:T(8,128)} %last.1) | copy-start | bytes 25165828

commit v2 on v1

--- a/solution.py
+++ b/solution.py
@@ -29,7 +29,7 @@
 
 
 class Tables:
-    def __init__(self, gx, gy, gz, modes, width):
+    def __init__(self, gx, gy, gz, modes, width, order):
         ay = angles(gy, retained(gy, modes))
         self.y = np.concatenate([np.cos(ay).T, np.sin(ay).T], 0).astype(np.float32)
         self.y_inv = np.concatenate([np.cos(ay), np.sin(ay)], 1).astype(np.float32)
@@ -48,7 +48,7 @@
             z_inv[1, d, :, d, 1] = -cz.T
         self.z = z.reshape(width * 2 * gz, 2 * width * modes).astype(np.float32)
         self.z_inv = z_inv.reshape(2 * width * modes, width * 2 * gz).astype(np.float32)
-        ax = angles(gx, retained(gx, modes))
+        ax = angles(gx, retained(gx, modes)[order])
         self.x = np.concatenate([np.cos(ax).T, np.sin(ax).T], 0).astype(np.float32)
         self.x_inv = np.concatenate([np.cos(ax), np.sin(ax)], 1).astype(np.float32)
 
@@ -143,42 +143,80 @@
     others = (net.count - 1) * local_planes
     drain(recv.at[pl.ds(0, others)], sems.at[1])
     table = table_ref[...]
-    groups, kl, fl, lanes = blocks.shape
-    half = lanes // 2
-    rows = groups * fl
+    _, width, rows, kl, tile = blocks.shape
+    tiles = rows // net.groups
+    half = recv.shape[2] // 2
+    modes = half // width
+    per = tile // modes
+    chunk = 8 if kl % 8 == 0 else kl
+
+    def source(c, k):
+        return blocks.at[:, :, pl.ds(c * tiles, tiles), pl.ds(k, chunk), :]
+
+    def target(c, k):
+        return out_ref.at[:, pl.ds(c * width, width), :, pl.ds(k, chunk), :]
+
     for k in range(kl):
         both = dot(table, recv[:, k, :])
-        cosine, sine = both[:rows], both[rows:]
+        cosine, sine = both[: per * rows], both[per * rows :]
         re = cosine[:, :half] + sine[:, half:]
         im = cosine[:, half:] - sine[:, :half]
-        value = jnp.concatenate([re, im], 1)
-        for c in range(groups):
-            blocks[c, k] = value[c * fl : (c + 1) * fl]
-        net.to_chan(
-            lambda c: blocks.at[c, k], lambda c: out_ref.at[c, k], sems.at[2], sems.at[3]
-        )
-    own = pltpu.make_async_copy(blocks.at[net.chan], out_ref.at[net.chan], sems.at[4])
+        for t, value in enumerate((re, im)):
+            for d in range(width):
+                lanes = slice(d * modes, (d + 1) * modes)
+                blocks[t, d, :, k, :] = jnp.concatenate(
+                    [value[j * rows : (j + 1) * rows, lanes] for j in range(per)], 1
+                )
+        if (k + 1) % chunk == 0:
+            start = k + 1 - chunk
+            net.to_chan(
+                lambda c: source(c, start), lambda c: target(c, start), sems.at[2], sems.at[3]
+            )
+    own = pltpu.make_async_copy(
+        blocks.at[:, :, pl.ds(net.chan * tiles, tiles), :, :],
+        out_ref.at[:, pl.ds(net.chan * width, width), :, :, :],
+        sems.at[4],
+    )
     own.start()
     own.wait()
     drain(send.at[pl.ds(0, others)], sems.at[0])
-    drain(blocks.at[pl.ds(0, groups - 1)], sems.at[2])
-    drain(out_ref.at[pl.ds(0, groups - 1)], sems.at[3])
+    drain(blocks.at[:, :, pl.ds(0, rows - tiles), :, :], sems.at[2])
+    drain(out_ref.at[:, pl.ds(0, (net.groups - 1) * width), :, :, :], sems.at[3])
 
 
 def start_synthesis(net, in_ref, table_ref, blocks, send, recv, sems, plane_sems, local_planes):
-    net.to_chan(
-        lambda c: in_ref.at[c], lambda c: blocks.at[c], sems.at[0], sems.at[1]
-    )
-    own = pltpu.make_async_copy(in_ref.at[net.chan], blocks.at[net.chan], sems.at[2])
+    _, width, rows, kl, tile = blocks.shape
+    tiles = rows // net.groups
+    half = recv.shape[2] // 2
+    modes = half // width
+    per = tile // modes
+
+    def source(c):
+        return in_ref.at[:, pl.ds(c * width, width), :, :, :]
+
+    def target(c):
+        return blocks.at[:, :, pl.ds(c * tiles, tiles), :, :]
+
+    net.to_chan(source, target, sems.at[0], sems.at[1])
+    own = pltpu.make_async_copy(source(net.chan), target(net.chan), sems.at[2])
     own.start()
     own.wait()
-    groups, kl, _, lanes = blocks.shape
-    drain(blocks.at[pl.ds(0, groups - 1)], sems.at[1])
+    drain(blocks.at[:, :, pl.ds(0, rows - tiles), :, :], sems.at[1])
     table = table_ref[...]
-    half = lanes // 2
     for k in range(kl):
-        value = jnp.concatenate([blocks[c, k] for c in range(groups)], 0)
-        turned = jnp.concatenate([-value[:, half:], value[:, :half]], 1)
+        loaded = [[blocks[t, d, :, k, :] for d in range(width)] for t in range(2)]
+        re, im = [
+            jnp.concatenate(
+                [
+                    jnp.concatenate([part[:, j * modes : (j + 1) * modes] for part in parts], 1)
+                    for j in range(per)
+                ],
+                0,
+            )
+            for parts in loaded
+        ]
+        value = jnp.concatenate([re, im], 1)
+        turned = jnp.concatenate([-im, re], 1)
         send[:, k, :] = dot(table, jnp.concatenate([value, turned], 0))
     mine = pl.ds(net.me * local_planes, local_planes)
     recv[mine] = send[mine]
@@ -191,7 +229,8 @@
 
 
 def finish_synthesis(net, in_ref, send, sems, local_planes):
-    drain(in_ref.at[pl.ds(0, net.groups - 1)], sems.at[0])
+    width = in_ref.shape[1] // net.groups
+    drain(in_ref.at[:, pl.ds(0, (net.groups - 1) * width), :, :, :], sems.at[0])
     drain(send.at[pl.ds(0, (net.count - 1) * local_planes)], sems.at[3])
 
 
@@ -363,54 +402,47 @@
 def mix_kernel(spec_ref, weight_ref, scale_ref, out_ref):
     channels = spec_ref.shape[1]
     scale = scale_ref[...]
+    spec = [(spec_ref[0, i, 0], spec_ref[1, i, 0]) for i in range(channels)]
 
     def one(o, carry):
-        re = jnp.zeros(spec_ref.shape[2:], F32)
+        re = jnp.zeros(spec_ref.shape[3:], F32)
         im = re
         for i in range(channels):
             wr, wi = weight_ref[0, i, o], weight_ref[1, i, o]
-            sr, si = spec_ref[0, i], spec_ref[1, i]
+            sr, si = spec[i]
             re = re + (sr * wr - si * wi)
             im = im + (sr * wi + si * wr)
-        out_ref[0, o] = re * scale
-        out_ref[1, o] = im * scale
+        out_ref[0, o, 0] = re * scale
+        out_ref[1, o, 0] = im * scale
         return carry
 
     lax.fori_loop(0, weight_ref.shape[2], one, 0)
 
 
-def back_kernel(grad_ref, weight_ref, scale_ref, out_ref):
+def back_kernel(
+    spec_ref, grad_ref, weight_ref, scale_ref, result_ref, out_ref, outer_ref, passed_ref
+):
     channels = grad_ref.shape[1]
     scale = scale_ref[...]
+    grads = [(grad_ref[0, o, 0] * scale, grad_ref[1, o, 0] * scale) for o in range(channels)]
+    passed_ref[...] = result_ref[...]
 
     def one(i, carry):
-        re = jnp.zeros(grad_ref.shape[2:], F32)
+        sr, si = spec_ref[0, i, 0], spec_ref[1, i, 0]
+        re = jnp.zeros(grad_ref.shape[3:], F32)
         im = re
         for o in range(channels):
             wr, wi = weight_ref[0, i, o], weight_ref[1, i, o]
-            gr, gi = grad_ref[0, o], grad_ref[1, o]
+            gr, gi = grads[o]
             re = re + (gr * wr + gi * wi)
             im = im + (gi * wr - gr * wi)
-        out_ref[0, i] = re * scale
-        out_ref[1, i] = im * scale
+            outer_ref[0, i, o] = sr * gr + si * gi
+            outer_ref[1, i, o] = sr * gi - si * gr
+        out_ref[0, i, 0] = re
+        out_ref[1, i, 0] = im
         return carry
 
     lax.fori_loop(0, weight_ref.shape[1], one, 0)
-
-
-def outer_kernel(spec_ref, grad_ref, scale_ref, out_ref):
-    channels = spec_ref.shape[1]
-    scale = scale_ref[...]
-
-    def one(i, carry):
-        sr, si = spec_ref[0, i] * scale, spec_ref[1, i] * scale
-        for o in range(channels):
-            gr, gi = grad_ref[0, o], grad_ref[1, o]
-            out_ref[0, i, o] = sr * gr + si * gi
-            out_ref[1, i, o] = sr * gi - si * gr
-        return carry
-
-    lax.fori_loop(0, channels, one, 0)
 
 
 def params(collective_id=None):
@@ -427,12 +459,6 @@
 
 def planes_spec(shape):
     return pl.BlockSpec((1, shape[1], 1, shape[3], shape[4]), lambda x: (0, 0, x, 0, 0))
-
-
-def modes_spec(shape):
-    tile = min(128, shape[-1])
-    lead = len(shape) - 1
-    return pl.BlockSpec(shape[:-1] + (tile,), lambda n: (0,) * lead + (n,))
 
 
 def shape_of(dims):
@@ -447,48 +473,42 @@
     fl = spec_weight.shape[4] // modes
     width = channels // groups
     lanes = 2 * width * modes
-    tables = Tables(gx, gy, gz, modes, width)
+    tile = min(128, fl * modes)
+    per, tiles = tile // modes, fl * modes // tile
+    order = np.arange(2 * modes).reshape(groups, tiles, per).transpose(2, 0, 1).reshape(-1)
+    tables = Tables(gx, gy, gz, modes, width, order)
     y, z, x = jnp.asarray(tables.y), jnp.asarray(tables.z), jnp.asarray(tables.x)
     y_inv, z_inv, x_inv = (
         jnp.asarray(tables.y_inv),
         jnp.asarray(tables.z_inv),
         jnp.asarray(tables.x_inv),
     )
-    weighting = np.where(np.arange(fl * modes) % modes == 0, 1.0, 2.0) / float(gx * gy * gz)
+    weighting = np.where(np.arange(tile) % modes == 0, 1.0, 2.0) / float(gx * gy * gz)
     scale = jnp.asarray(weighting.astype(np.float32)[None, :])
-    block_shape = (groups, kl, fl, lanes)
-    mode_shape = (2, channels, kl, fl * modes)
+    mode_shape = (2, channels, tiles, kl, tile)
     plane_rows = pltpu.VMEM((gx, kl, lanes), F32)
-    mode_rows = pltpu.VMEM(block_shape, F32)
+    mode_rows = pltpu.VMEM((2, width, groups * tiles, kl, tile), F32)
     semaphores = pltpu.SemaphoreType.DMA((5,))
     plane_semaphores = pltpu.SemaphoreType.DMA((local_planes,))
     anywhere = pl.BlockSpec(memory_space=pl.ANY)
     smem = pl.BlockSpec(memory_space=pltpu.SMEM)
     plane_block = planes_spec(field.shape)
 
-    def to_modes(blocks):
-        blocks = blocks.reshape(groups, kl, fl, 2, width, modes)
-        return blocks.transpose(3, 0, 4, 1, 2, 5).reshape(mode_shape)
-
-    def from_modes(mixed):
-        blocks = mixed.reshape(2, groups, width, kl, fl, modes).transpose(1, 3, 4, 0, 2, 5)
-        return blocks.reshape(block_shape)
-
-    blocks = pl.pallas_call(
+    spectrum = pl.pallas_call(
         functools.partial(first_kernel, plane_count, groups),
         grid=(local_planes,),
         in_specs=[plane_block, whole(y), whole(z), whole(x)],
         out_specs=anywhere,
-        out_shape=shape_of(block_shape),
+        out_shape=shape_of(mode_shape),
         scratch_shapes=[plane_rows, plane_rows, mode_rows, semaphores],
         compiler_params=params(1),
         name="first",
     )(field, y, z, x)
-    spectrum = to_modes(blocks)
-    mode_block = modes_spec(mode_shape)
-    weight_block = modes_spec(spec_weight.shape)
-    scale_block = modes_spec(scale.shape)
-    mode_grid = (mode_shape[-1] // min(128, mode_shape[-1]),)
+    rows = 8 if kl % 8 == 0 else kl
+    mode_grid = (tiles, kl // rows)
+    mode_block = pl.BlockSpec((2, channels, 1, rows, tile), lambda n, k: (0, 0, n, k, 0))
+    weight_block = pl.BlockSpec((2, channels, channels, rows, tile), lambda n, k: (0, 0, 0, k, n))
+    scale_block = whole(scale)
     mixed = pl.pallas_call(
         mix_kernel,
         grid=mode_grid,
@@ -498,13 +518,13 @@
         compiler_params=params(),
         name="mix",
     )(spectrum, spec_weight, scale)
-    output, local_grad, blocks = pl.pallas_call(
+    output, local_grad, grad_modes = pl.pallas_call(
         functools.partial(middle_kernel, plane_count, groups),
         grid=(local_planes,),
         in_specs=[smem, smem, anywhere, plane_block, plane_block]
         + [whole(y_inv), whole(z_inv), whole(x_inv), whole(y), whole(z), whole(x)],
         out_specs=[plane_block, plane_block, anywhere],
-        out_shape=[shape_of(field.shape), shape_of(field.shape), shape_of(block_shape)],
+        out_shape=[shape_of(field.shape), shape_of(field.shape), shape_of(mode_shape)],
         scratch_shapes=[pltpu.VMEM((gy, channels * gz), F32)] * 2
         + [mode_rows, plane_rows, plane_rows, semaphores, plane_semaphores]
         + [plane_rows, plane_rows, mode_rows, semaphores],
@@ -513,7 +533,7 @@
     )(
         point_weight,
         bias,
-        from_modes(mixed),
+        mixed,
         field,
         cotangent,
         y_inv,
@@ -523,25 +543,21 @@
         z,
         x,
     )
-    grad_modes = to_modes(blocks)
-    spectrum_grad = pl.pallas_call(
+    steps = tiles * (kl // rows)
+    flat = output.reshape(-1, gz)
+    flat_block = pl.BlockSpec(
+        (flat.shape[0] // steps, gz), lambda n, k: (n * (kl // rows) + k, 0)
+    )
+    spectrum_grad, weight_grad, flat = pl.pallas_call(
         back_kernel,
         grid=mode_grid,
-        in_specs=[mode_block, weight_block, scale_block],
-        out_specs=mode_block,
-        out_shape=shape_of(mode_shape),
+        in_specs=[mode_block, mode_block, weight_block, scale_block, flat_block],
+        out_specs=[mode_block, weight_block, flat_block],
+        out_shape=[shape_of(mode_shape), shape_of(spec_weight.shape), shape_of(flat.shape)],
         compiler_params=params(),
         name="back",
-    )(grad_modes, spec_weight, scale)
-    weight_grad = pl.pallas_call(
-        outer_kernel,
-        grid=mode_grid,
-        in_specs=[mode_block, mode_block, scale_block],
-        out_specs=weight_block,
-        out_shape=shape_of(spec_weight.shape),
-        compiler_params=params(),
-        name="weight_grad",
-    )(spectrum, grad_modes, scale)
+    )(spectrum, grad_modes, spec_weight, scale, flat)
+    output = flat.reshape(output.shape)
     field_grad = pl.pallas_call(
         functools.partial(last_kernel, plane_count, groups),
         grid=(local_planes,),
@@ -551,7 +567,7 @@
         scratch_shapes=[mode_rows, plane_rows, plane_rows, semaphores, plane_semaphores],
         compiler_params=params(3),
         name="last",
-    )(from_modes(spectrum_grad), local_grad, y_inv, z_inv, x_inv)
+    )(spectrum_grad, local_grad, y_inv, z_inv, x_inv)
     return (output, field_grad, weight_grad)
 
 

time: 399 us -> 343 us (0.86)
  local copies, waits for them, and re-layouts: 70 us -> 7.89 us
  Pallas kernels: 328 us -> 334 us
    reshape x12 -> x0, local copies, waits for them, and re-layouts: 58.6 us -> none  [the longest x4 21.3 us: from_modes(): mixed.reshape(2, groups, width, kl, fl, modes).transpose(1, 3, 4, 0, 2, 5)]
    pallas_call x2 -> x1, Pallas kernels: 16.3 us -> 20.9 us  [local(): pl.pallas_call(back_kernel, grid=mode_grid, in_specs=[mode_block, mode_bl...]
    unnamed x4 -> x1, local copies, waits for them, and re-layouts: 11.4 us -> 7.89 us
where the time goes in v2:
time: 343 us
  Pallas kernels  334 us (97%)
  local copies, waits for them, and re-layouts  7.89 us (2%)
    pallas_call x1, Pallas kernels, local(): pl.pallas_call(functools.partial(middle_kernel, plane_count, groups), gri...  146 us
    pallas_call x1, Pallas kernels, local(): pl.pallas_call(functools.partial(first_kernel, plane_count, groups), grid...  78.5 us
    pallas_call x1, Pallas kernels, local(): pl.pallas_call(functools.partial(last_kernel, plane_count, groups), grid=...  77.7 us
    pallas_call x1, Pallas kernels, local(): pl.pallas_call(back_kernel, grid=mode_grid, in_specs=[mode_block, mode_bl...  20.9 us
    pallas_call x1, Pallas kernels, local(): pl.pallas_call(mix_kernel, grid=mode_grid, in_specs=[mode_block, weight_b...  10.9 us
    unnamed x1, local copies, waits for them, and re-layouts  7.89 us

profile of v2, /device:TPU:0, one launch (start us, length us, event | category | flops | bytes accessed | tf_op | source)
XLA Modules:
  0.0 342.6 jit_solution(3558686928808196024)
XLA Ops:
  0.6 78.5 %first.1.spec_ref = f32[2,16,4,16,128]{4,3,2,1,0:T(8,128)} custom-call(f32[1,16,8,128,128]{4,3,2,1,0:T(8,128)} %field_ref.3, f32[128,128]{1,0:T(8,128)} %constant.14.clone.y_ref, f32[1024,256]{1,0:T(8,128)} %constant.15.clone.z_ref, f32[128,128]{1,0:T(8,128)} %constant.16.clone.x_ref), custom_call_target="tpu_custom_call" | custom-call | tf_op jit(solution)/shard_map/first/pallas_call | solution.py:497
  79.2 10.9 %mix.1.in_ref = f32[2,16,4,16,128]{4,3,2,1,0:T(8,128)} custom-call(f32[2,16,4,16,128]{4,3,2,1,0:T(8,128)} %first.1.spec_ref, f32[2,16,16,16,512]{4,3,2,1,0:T(8,128)} %weight_ref.5, f32[1,128]{1,0:T(1,128)} %constant.20.clone.scale_ref), custom_call_target="tpu_custom_call" | custom-call | tf_op jit(solution)/shard_map/mix/pallas_call | solution.py:512
  90.1 146.1 %middle.1 = (f32[1,16,8,128,128]{4,3,2,1,0:T(8,128)}, f32[1,16,8,128,128]{4,3,2,1,0:T(8,128)}, f32[2,16,4,16,128]{4,3,2,1,0:T(8,128)}) custom-call(f32[16,16]{1,0:T(8,128)} %weight_ref.4, f32[16]{0:T(128)} %bias_ref.1, f32[2,16,4,16,128]{4,3,2,1,0:T(8,128)} %mix.1.in_ref, f32[1,16,8,128,128]{4,3,2,1,0:T(8,128)} %field_ref.3, ...), custom_call_target="tpu_custom_call" | custom-call | tf_op jit(solution)/shard_map/middle/pallas_call | solution.py:521
  236.1 20.9 %back.1 = (f32[2,16,4,16,128]{4,3,2,1,0:T(8,128)}, f32[2,16,16,16,512]{4,3,2,1,0:T(8,128)}, f32[16384,128]{1,0:T(8,128)}) custom-call(f32[2,16,4,16,128]{4,3,2,1,0:T(8,128)} %first.1.spec_ref, f32[2,16,4,16,128]{4,3,2,1,0:T(8,128)} %get-tuple-element.9.grad_ref, f32[2,16,16,16,512]{4,3,2,1,0:T(8,128)} %weight_ref.5, f32[1,128]{1,0:T(1,128)} %constant.20.clone.scale_ref, ...), custom_call_target="tpu_custom_call" | custom-call | tf_op jit(solution)/shard_map/back/pallas_call | solution.py:551
  257.0 77.7 %last.1 = f32[1,16,8,128,128]{4,3,2,1,0:T(8,128)} custom-call(f32[2,16,4,16,128]{4,3,2,1,0:T(8,128)} %get-tuple-element.12.in_ref, f32[1,16,8,128,128]{4,3,2,1,0:T(8,128)} %get-tuple-element.13.grad_ref, f32[128,128]{1,0:T(8,128)} %constant.17.clone.y_inv_ref, f32[256,1024]{1,0:T(8,128)} %constant.18.clone.z_inv_ref, f32[128,128]{1,0:T(8,128)} %constant.19.clone.x_inv_ref), custom_call_target="tpu_custom_call" | custom-call | tf_op jit(solution)/shard_map/last/pallas_call | solution.py:561
  334.7 7.9 %copy.16 = f32[1,16,8,128,128]{4,3,2,1,0:T(8,128)} copy(f32[1,16,8,128,128]{4,3,2,1,0:T(8,128)} %last.1) | data formatting | bytes 16777216

commit v3 on v2

--- a/solution.py
+++ b/solution.py
@@ -93,12 +93,12 @@
         lax.fori_loop(1, self.count, greet, 0)
         pl.semaphore_wait(semaphore, self.count - 1)
 
-    def to_all(self, source, target, local_planes, x, send, recv):
+    def to_all(self, source, target, local_planes, x, ky, send, recv):
         def one(offset, carry):
             other = lax.rem(self.me + offset, self.count)
             pltpu.make_async_remote_copy(
-                src_ref=source.at[other * local_planes + x],
-                dst_ref=target.at[self.me * local_planes + x],
+                src_ref=source.at[other * local_planes + x, ky, :],
+                dst_ref=target.at[self.me * local_planes + x, ky, :],
                 send_sem=send,
                 recv_sem=recv,
                 device_id={"planes": other // self.groups, "chan": lax.rem(other, self.groups)},
@@ -124,11 +124,16 @@
         lax.fori_loop(1, self.groups, one, 0)
 
 
+def pieces(kl):
+    size = 8 if kl % 8 == 0 else kl
+    return [pl.ds(start, size) for start in range(0, kl, size)]
+
+
 def drain(ref, semaphore):
     pltpu.make_async_copy(ref, ref, semaphore).wait()
 
 
-def send_plane(net, result, x, local_planes, kl, send, recv, sems):
+def send_plane(net, result, x, local_planes, kl, send, recv, sems, hold):
     rows = net.count // net.groups * kl
     for c in range(net.groups):
         for p in range(net.count // net.groups):
@@ -136,12 +141,25 @@
             send[(p * net.groups + c) * local_planes + x] = result[start : start + kl]
     mine = net.me * local_planes + x
     recv[mine] = send[mine]
-    net.to_all(send, recv, local_planes, x, sems.at[0], sems.at[1])
-
-
-def finish_analysis(net, table_ref, out_ref, send, recv, blocks, sems, local_planes):
+    cuts = pieces(kl) if hold else [pl.ds(0, kl)]
+    for h, ky in enumerate(cuts[:1]):
+        net.to_all(send, recv, local_planes, x, ky, sems.at[0], sems.at[5 + h])
+    if len(cuts) == 1:
+        return
+
+    @pl.when(x == local_planes - 1)
+    def _():
+        for h, ky in list(enumerate(cuts))[1:]:
+
+            def plane(row, carry):
+                net.to_all(send, recv, local_planes, row, ky, sems.at[0], sems.at[5 + h])
+                return carry
+
+            lax.fori_loop(0, local_planes, plane, 0)
+
+
+def finish_analysis(net, table_ref, out_ref, send, recv, blocks, sems, local_planes, hold):
     others = (net.count - 1) * local_planes
-    drain(recv.at[pl.ds(0, others)], sems.at[1])
     table = table_ref[...]
     _, width, rows, kl, tile = blocks.shape
     tiles = rows // net.groups
@@ -149,6 +167,7 @@
     modes = half // width
     per = tile // modes
     chunk = 8 if kl % 8 == 0 else kl
+    piece = chunk if hold else kl
 
     def source(c, k):
         return blocks.at[:, :, pl.ds(c * tiles, tiles), pl.ds(k, chunk), :]
@@ -157,6 +176,8 @@
         return out_ref.at[:, pl.ds(c * width, width), :, pl.ds(k, chunk), :]
 
     for k in range(kl):
+        if k % piece == 0:
+            drain(recv.at[pl.ds(0, others), pl.ds(k, piece), :], sems.at[5 + k // piece])
         both = dot(table, recv[:, k, :])
         cosine, sine = both[: per * rows], both[per * rows :]
         re = cosine[:, :half] + sine[:, half:]
@@ -184,26 +205,44 @@
     drain(out_ref.at[:, pl.ds(0, (net.groups - 1) * width), :, :, :], sems.at[3])
 
 
-def start_synthesis(net, in_ref, table_ref, blocks, send, recv, sems, plane_sems, local_planes):
+def start_synthesis(
+    net, in_ref, table_ref, blocks, send, recv, sems, plane_sems, local_planes, early
+):
     _, width, rows, kl, tile = blocks.shape
     tiles = rows // net.groups
     half = recv.shape[2] // 2
     modes = half // width
     per = tile // modes
 
-    def source(c):
-        return in_ref.at[:, pl.ds(c * width, width), :, :, :]
-
-    def target(c):
-        return blocks.at[:, :, pl.ds(c * tiles, tiles), :, :]
-
-    net.to_chan(source, target, sems.at[0], sems.at[1])
-    own = pltpu.make_async_copy(source(net.chan), target(net.chan), sems.at[2])
+    def source(c, ky):
+        return in_ref.at[:, pl.ds(c * width, width), :, ky, :]
+
+    def target(c, ky):
+        return blocks.at[:, :, pl.ds(c * tiles, tiles), ky, :]
+
+    cuts = pieces(kl)
+    size = kl // len(cuts)
+    for h, ky in enumerate(cuts):
+        net.to_chan(
+            lambda c: source(c, ky), lambda c: target(c, ky), sems.at[0], sems.at[5 + h]
+        )
+    every = pl.ds(0, kl)
+    own = pltpu.make_async_copy(source(net.chan, every), target(net.chan, every), sems.at[2])
     own.start()
     own.wait()
-    drain(blocks.at[:, :, pl.ds(0, rows - tiles), :, :], sems.at[1])
     table = table_ref[...]
+
+    def send_planes(ky):
+        def plane(x, carry):
+            net.to_all(send, recv, local_planes, x, ky, sems.at[3], plane_sems.at[x])
+            return carry
+
+        lax.fori_loop(0, local_planes, plane, 0)
+
     for k in range(kl):
+        if k % size == 0:
+            h = k // size
+            drain(blocks.at[:, :, pl.ds(0, rows - tiles), cuts[h], :], sems.at[5 + h])
         loaded = [[blocks[t, d, :, k, :] for d in range(width)] for t in range(2)]
         re, im = [
             jnp.concatenate(
@@ -218,14 +257,12 @@
         value = jnp.concatenate([re, im], 1)
         turned = jnp.concatenate([-im, re], 1)
         send[:, k, :] = dot(table, jnp.concatenate([value, turned], 0))
+        if early and (k + 1) % size == 0:
+            send_planes(cuts[k // size])
+    if not early:
+        send_planes(every)
     mine = pl.ds(net.me * local_planes, local_planes)
     recv[mine] = send[mine]
-
-    def plane(x, carry):
-        net.to_all(send, recv, local_planes, x, sems.at[3], plane_sems.at[x])
-        return carry
-
-    lax.fori_loop(0, local_planes, plane, 0)
 
 
 def finish_synthesis(net, in_ref, send, sems, local_planes):
@@ -268,11 +305,11 @@
     channels = field_ref.shape[1]
     planes = jnp.concatenate([field_ref[0, i, 0] for i in range(channels)], 1)
     result = analysis_rows(planes, y_ref[...], z_ref[...], channels, groups)
-    send_plane(net, result, x, local_planes, recv.shape[1], send, recv, sems)
+    send_plane(net, result, x, local_planes, recv.shape[1], send, recv, sems, True)
 
     @pl.when(x == local_planes - 1)
     def _():
-        finish_analysis(net, x_ref, out_ref, send, recv, blocks, sems, local_planes)
+        finish_analysis(net, x_ref, out_ref, send, recv, blocks, sems, local_planes, True)
 
 
 def middle_kernel(
@@ -321,6 +358,7 @@
             back_sems,
             plane_sems,
             local_planes,
+            False,
         )
 
     drain(back_recv.at[pl.ds(0, net.count - 1)], plane_sems.at[x])
@@ -353,11 +391,11 @@
 
     lax.fori_loop(0, gy // step, chunk, 0)
     result = analysis_rows(pre_grad[...], y_ref[...], z_ref[...], channels, groups)
-    send_plane(net, result, x, local_planes, recv.shape[1], send, recv, sems)
+    send_plane(net, result, x, local_planes, recv.shape[1], send, recv, sems, False)
 
     @pl.when(x == local_planes - 1)
     def _():
-        finish_analysis(net, x_ref, next_ref, send, recv, blocks, sems, local_planes)
+        finish_analysis(net, x_ref, next_ref, send, recv, blocks, sems, local_planes, False)
         finish_synthesis(net, in_ref, back_send, back_sems, local_planes)
 
 
@@ -384,7 +422,7 @@
     def _():
         net.barrier()
         start_synthesis(
-            net, in_ref, x_inv_ref, blocks, send, recv, sems, plane_sems, local_planes
+            net, in_ref, x_inv_ref, blocks, send, recv, sems, plane_sems, local_planes, True
         )
 
     drain(recv.at[pl.ds(0, net.count - 1)], plane_sems.at[x])
@@ -488,7 +526,7 @@
     mode_shape = (2, channels, tiles, kl, tile)
     plane_rows = pltpu.VMEM((gx, kl, lanes), F32)
     mode_rows = pltpu.VMEM((2, width, groups * tiles, kl, tile), F32)
-    semaphores = pltpu.SemaphoreType.DMA((5,))
+    semaphores = pltpu.SemaphoreType.DMA((5 + kl,))
     plane_semaphores = pltpu.SemaphoreType.DMA((local_planes,))
     anywhere = pl.BlockSpec(memory_space=pl.ANY)
     smem = pl.BlockSpec(memory_space=pltpu.SMEM)

time: 343 us -> 343 us (level)
  no operation moved by 1% of the time
where the time goes in v3:
time: 343 us; the launch traced here: 342 us
  Pallas kernels  334 us (97%)
  local copies, waits for them, and re-layouts  7.89 us (2%)
    pallas_call x1, Pallas kernels, local(): pl.pallas_call(functools.partial(middle_kernel, plane_count, groups), gri...  149 us
    pallas_call x1, Pallas kernels, local(): pl.pallas_call(functools.partial(last_kernel, plane_count, groups), grid=...  77.8 us
    pallas_call x1, Pallas kernels, local(): pl.pallas_call(functools.partial(first_kernel, plane_count, groups), grid...  75.3 us
    pallas_call x1, Pallas kernels, local(): pl.pallas_call(back_kernel, grid=mode_grid, in_specs=[mode_block, mode_bl...  20.9 us
    pallas_call x1, Pallas kernels, local(): pl.pallas_call(mix_kernel, grid=mode_grid, in_specs=[mode_block, weight_b...  10.9 us
    unnamed x1, local copies, waits for them, and re-layouts  7.89 us

profile of v3, /device:TPU:0, one launch (start us, length us, event | category | flops | bytes accessed | tf_op | source)
XLA Modules:
  0.0 342.1 jit_solution(6617338091514176995)
XLA Ops:
  0.6 75.3 %first.1.spec_ref = f32[2,16,4,16,128]{4,3,2,1,0:T(8,128)} custom-call(f32[1,16,8,128,128]{4,3,2,1,0:T(8,128)} %field_ref.3, f32[128,128]{1,0:T(8,128)} %constant.14.clone.y_ref, f32[1024,256]{1,0:T(8,128)} %constant.15.clone.z_ref, f32[128,128]{1,0:T(8,128)} %constant.16.clone.x_ref), custom_call_target="tpu_custom_call" | custom-call | tf_op jit(solution)/shard_map/first/pallas_call | solution.py:535
  76.0 10.9 %mix.1.in_ref = f32[2,16,4,16,128]{4,3,2,1,0:T(8,128)} custom-call(f32[2,16,4,16,128]{4,3,2,1,0:T(8,128)} %first.1.spec_ref, f32[2,16,16,16,512]{4,3,2,1,0:T(8,128)} %weight_ref.5, f32[1,128]{1,0:T(1,128)} %constant.20.clone.scale_ref), custom_call_target="tpu_custom_call" | custom-call | tf_op jit(solution)/shard_map/mix/pallas_call | solution.py:550
  86.8 148.7 %middle.1 = (f32[1,16,8,128,128]{4,3,2,1,0:T(8,128)}, f32[1,16,8,128,128]{4,3,2,1,0:T(8,128)}, f32[2,16,4,16,128]{4,3,2,1,0:T(8,128)}) custom-call(f32[16,16]{1,0:T(8,128)} %weight_ref.4, f32[16]{0:T(128)} %bias_ref.1, f32[2,16,4,16,128]{4,3,2,1,0:T(8,128)} %mix.1.in_ref, f32[1,16,8,128,128]{4,3,2,1,0:T(8,128)} %field_ref.3, ...), custom_call_target="tpu_custom_call" | custom-call | tf_op jit(solution)/shard_map/middle/pallas_call | solution.py:559
  235.6 20.9 %back.1 = (f32[2,16,4,16,128]{4,3,2,1,0:T(8,128)}, f32[2,16,16,16,512]{4,3,2,1,0:T(8,128)}, f32[16384,128]{1,0:T(8,128)}) custom-call(f32[2,16,4,16,128]{4,3,2,1,0:T(8,128)} %first.1.spec_ref, f32[2,16,4,16,128]{4,3,2,1,0:T(8,128)} %get-tuple-element.9.grad_ref, f32[2,16,16,16,512]{4,3,2,1,0:T(8,128)} %weight_ref.5, f32[1,128]{1,0:T(1,128)} %constant.20.clone.scale_ref, ...), custom_call_target="tpu_custom_call" | custom-call | tf_op jit(solution)/shard_map/back/pallas_call | solution.py:589
  256.4 77.8 %last.1 = f32[1,16,8,128,128]{4,3,2,1,0:T(8,128)} custom-call(f32[2,16,4,16,128]{4,3,2,1,0:T(8,128)} %get-tuple-element.12.in_ref, f32[1,16,8,128,128]{4,3,2,1,0:T(8,128)} %get-tuple-element.13.grad_ref, f32[128,128]{1,0:T(8,128)} %constant.17.clone.y_inv_ref, f32[256,1024]{1,0:T(8,128)} %constant.18.clone.z_inv_ref, f32[128,128]{1,0:T(8,128)} %constant.19.clone.x_inv_ref), custom_call_target="tpu_custom_call" | custom-call | tf_op jit(solution)/shard_map/last/pallas_call | solution.py:599
  334.2 7.9 %copy.16 = f32[1,16,8,128,128]{4,3,2,1,0:T(8,128)} copy(f32[1,16,8,128,128]{4,3,2,1,0:T(8,128)} %last.1) | data formatting | bytes 16777216
